TPU v7x, 32 devices: a whole 2x2x4 slice. The times are simulated.
32 devices in a mesh: dp: 8 (over y, x, core), tensor: 4 (over z).
Axes of the slice: x: 2, y: 2, z: 4, core: 2. Of those that a mesh axis runs over, the one named last changes fastest.
Arguments:
- tokens: bfloat16 [4096, 768], P('dp'), may hold values from -6 to 6
- segment_ids: int32 [8, 512], P('dp'), may hold values from 0 to 1, never falling along the last dimension, each value on 1 to 320 neighbouring positions
- visible: int32 [8, 512], P('dp'), may hold values 0 or 1
- mask_index: int32 [8, 320], P('dp'), may hold values from 0 to 511, as said below
- targets: float32 [8, 320, 16], P('dp'), may hold values from -6 to 6
- noise: float32 [4, 8, 320, 16], P(None, 'dp'), may hold values from -6 to 6
- timesteps: int32 [4, 8, 320], P(None, 'dp'), may hold values from 1 to 998
- ln1_gain: float32 [768], replicated, may hold values from 0.5 to 1.5
- ln1_bias: float32 [768], replicated, may hold values from -3 to 3
- qkv_weight: bfloat16 [768, 3, 768], P(None, None, 'tensor'), may hold values from -0.21875 to 0.21875
- proj_weight: bfloat16 [768, 768], P('tensor'), may hold values from -1.75 to 1.75
- ln2_gain: float32 [768], replicated, may hold values from 0.5 to 1.5
- ln2_bias: float32 [768], replicated, may hold values from -3 to 3
- fc_in_weight: bfloat16 [768, 3072], P(None, 'tensor'), may hold values from -0.21875 to 0.21875
- fc_out_weight: bfloat16 [3072, 768], P('tensor'), may hold values from -0.109375 to 0.109375
- cond_weight: bfloat16 [768, 1024], replicated, may hold values from -0.21875 to 0.21875
- time_in_weight: bfloat16 [256, 1024], replicated, may hold values from -0.5 to 0.5
- time_out_weight: bfloat16 [1024, 1024], replicated, may hold values from -0.1875 to 0.1875
- input_weight: bfloat16 [16, 1024], P(None, 'tensor'), may hold values from -1.5 to 1.5
- ada_weight: bfloat16 [6, 1024, 3, 1024], P(None, None, None, 'tensor'), may hold values from -0.09375 to 0.09375
- block_in_weight: bfloat16 [6, 1024, 1024], P(None, None, 'tensor'), may hold values from -0.1875 to 0.1875
- block_out_weight: bfloat16 [6, 1024, 1024], P(None, 'tensor'), may hold values from -0.1875 to 0.1875
- final_ada_weight: bfloat16 [1024, 2, 1024], P(None, None, 'tensor'), may hold values from -0.09375 to 0.09375
- out_weight: bfloat16 [1024, 32], P('tensor'), may hold values from -0.1875 to 0.1875
Outputs:
- loss: float32 [], replicated
- hidden_out: bfloat16 [4096, 768], P('dp')
- input_grad: float32 [4096, 768], P('dp')
- ln1_gain_grad: float32 [768], replicated
- ln1_bias_grad: float32 [768], replicated
- qkv_grad: float32 [768, 3, 768], P('dp', None, 'tensor')
- proj_grad: float32 [768, 768], P('tensor', 'dp')
- ln2_gain_grad: float32 [768], replicated
- ln2_bias_grad: float32 [768], replicated
- fc_in_grad: float32 [768, 3072], P('dp', 'tensor')
- fc_out_grad: float32 [3072, 768], P('tensor', 'dp')
- cond_grad: float32 [768, 1024], P('dp')
- time_in_grad: float32 [256, 1024], P('dp')
- time_out_grad: float32 [1024, 1024], P('dp')
- input_weight_grad: float32 [16, 1024], P(None, 'tensor')
- ada_grad: float32 [6, 1024, 3, 1024], P(None, 'dp', None, 'tensor')
- block_in_grad: float32 [6, 1024, 1024], P(None, 'dp', 'tensor')
- block_out_grad: float32 [6, 1024, 1024], P(None, 'tensor', 'dp')
- final_ada_grad: float32 [1024, 2, 1024], P('dp', None, 'tensor')
- out_weight_grad: float32 [1024, 32], P('tensor')
Inputs may be any that keep to these rules, and one draw needn't show every extreme that they name: `segment_ids`: within a row (one sequence) an image is a run of consecutive positions of at most 320 tokens, numbered in order. `mask_index`: each row holds 320 distinct positions of that sequence in increasing order.
All inputs are finite; a program needn't handle non-finite values. No bound on the sum of `visible` on one device may be relied on, other than what follows from the above.
Results may differ from a plain program's by a relative error of at most 0.02.
The roundings to bfloat16 on the way count: a program that leaves them out, or rounds other values in their place, can miss the bound.
Values may be sent and summed in bfloat16 or wider, within the bound.
A program may use at most 320 MiB of HBM per device.

v0:
```python
from functools import partial
import math

import jax
import jax.numpy as jnp
from jax import lax
from jax.sharding import PartitionSpec as P

HEAD = 64
HW = 1024
DEPTH = 6
TOKCH = 16
FREQ = 256
COPIES = 4
STEPS = 1000


norm_eps = 1e-06


def product(left_op, right_op):
    return jnp.dot(left_op, right_op, preferred_element_type=jnp.float32)


def branch_total(partial_sums):
    return lax.psum(partial_sums, "tensor")


def row_sums(first_sum, second_sum):
    return lax.psum((first_sum, second_sum), "tensor")


def affine_norm(values, gain_vec, offset):
    centred = values - jnp.mean(values, axis=-1, keepdims=True)
    inverse = lax.rsqrt(jnp.mean(centred * centred, axis=-1, keepdims=True) + norm_eps)
    normal = centred * inverse
    return (normal * gain_vec + offset, normal, inverse)


def affine_back(grad_out, normal, inverse, gain_vec):
    scaled = grad_out * gain_vec
    centred = (
        scaled
        - jnp.mean(scaled, axis=-1, keepdims=True)
        - normal * jnp.mean(scaled * normal, axis=-1, keepdims=True)
    )
    return (inverse * centred, jnp.sum(grad_out * normal, axis=0), jnp.sum(grad_out, axis=0))


def sharded_norm(residual):
    moment_one, moment_two = row_sums(
        jnp.sum(residual, axis=-1, keepdims=True),
        jnp.sum(residual * residual, axis=-1, keepdims=True),
    )
    row_mean = moment_one / HW
    inverse = lax.rsqrt(moment_two / HW - row_mean * row_mean + norm_eps)
    return ((residual - row_mean) * inverse, inverse)


def sharded_back(grad_normal, normal, inverse):
    moment_one, moment_two = row_sums(
        jnp.sum(grad_normal, axis=-1, keepdims=True),
        jnp.sum(grad_normal * normal, axis=-1, keepdims=True),
    )
    return inverse * (grad_normal - moment_one / HW - normal * moment_two / HW)


def plan(time_rows):
    moment = time_rows.astype(jnp.float32)
    quarter = math.pi / 2.0
    angle_zero = 0.008 / 1.008 * quarter
    angle_now = ((moment + 1.0) / STEPS + 0.008) / 1.008 * quarter
    angle_prev = (moment / STEPS + 0.008) / 1.008 * quarter
    start_level = math.cos(angle_zero) ** 2
    abar_now = jnp.cos(angle_now) ** 2 / start_level
    abar_prev = jnp.cos(angle_prev) ** 2 / start_level
    one_minus_now = jnp.sin(angle_now - angle_zero) * jnp.sin(angle_now + angle_zero) / start_level
    one_minus_prev = (
        jnp.sin(angle_prev - angle_zero) * jnp.sin(angle_prev + angle_zero) / start_level
    )
    beta_step = (
        jnp.sin(angle_now - angle_prev) * jnp.sin(angle_now + angle_prev) / jnp.cos(angle_prev) ** 2
    )
    alpha_step = abar_now / abar_prev
    beta_tilde = beta_step * one_minus_prev / one_minus_now
    return (abar_now, alpha_step, beta_step, beta_tilde, one_minus_now)


def frequency(time_rows):
    half_width = FREQ // 2
    freq_rates = jnp.exp(
        -math.log(10000.0) * jnp.arange(half_width).astype(jnp.float32) / half_width
    )
    angles = time_rows.astype(jnp.float32)[:, None] * freq_rates[None, :]
    return jnp.concatenate([jnp.cos(angles), jnp.sin(angles)], axis=-1)


def loss_rows(predicted, eps_true, beta_step, beta_tilde, coef_diff):
    eps_pred = predicted[:, :TOKCH]
    var_raw = predicted[:, TOKCH:]
    squared = jnp.mean((eps_true - eps_pred) ** 2, axis=-1)
    fraction = (var_raw + 1.0) / 2.0
    log_tilde = jnp.log(beta_tilde)
    log_model = fraction * jnp.log(beta_step) + (1.0 - fraction) * log_tilde
    mean_gap = coef_diff * (eps_pred - eps_true)
    diverge = 0.5 * (
        -1.0
        + log_model
        - log_tilde
        + jnp.exp(log_tilde - log_model)
        + mean_gap * mean_gap * jnp.exp(-log_model)
    )
    return squared + jnp.mean(diverge, axis=-1) / math.log(2.0)


def shards(
    tokens,
    segment_ids,
    visible,
    mask_index,
    targets,
    noise,
    timesteps,
    ln1_gain,
    ln1_bias,
    qkv_weight,
    proj_weight,
    ln2_gain,
    ln2_bias,
    fc_in_weight,
    fc_out_weight,
    cond_weight,
    time_in_weight,
    time_out_weight,
    input_weight,
    ada_weight,
    block_in_weight,
    block_out_weight,
    final_ada_weight,
    out_weight,
):
    token_count, model_width = tokens.shape
    local_width = qkv_weight.shape[2]
    head_count = local_width // HEAD
    score_scale = 1.0 / math.sqrt(HEAD)
    block_rows = min(512, token_count)
    inputs = tokens.astype(jnp.float32)
    normed_one, normal_one, inverse_one = affine_norm(inputs, ln1_gain, ln1_bias)
    attn_in = normed_one.astype(jnp.bfloat16)
    qkv_flat = qkv_weight.reshape(model_width, 3 * local_width)
    projected = product(attn_in, qkv_flat).astype(jnp.bfloat16)
    queries = projected[:, :local_width].reshape(token_count, head_count, HEAD)
    key_rows = projected[:, local_width : 2 * local_width].reshape(token_count, head_count, HEAD)
    value_rows = projected[:, 2 * local_width :].reshape(token_count, head_count, HEAD)
    segments = segment_ids[0]
    shown_keys = visible[0]
    positions = jnp.arange(token_count)

    def block_scores(start_row):
        query_pos = start_row + jnp.arange(block_rows)
        allowed = (segments[:, None] == segments[None, :]) & (
            (shown_keys[None, :] == 1) | (query_pos[:, None] == positions[None, :])
        )
        scores = (
            jnp.einsum("qhd,khd->hqk", queries, key_rows, preferred_element_type=jnp.float32)
            * score_scale
        )
        return jnp.where(allowed[None], scores, -1e30)

    start_row = 0
    scores = block_scores(start_row)
    row_top = jnp.max(scores, axis=-1, keepdims=True)
    weights_exp = jnp.exp(scores - row_top)
    row_total = jnp.sum(weights_exp, axis=-1, keepdims=True)
    probability = (weights_exp / row_total).astype(jnp.bfloat16)
    log_totals = [row_top + jnp.log(row_total)]
    pieces_out = jnp.einsum(
        "hqk,khd->qhd", probability, value_rows, preferred_element_type=jnp.float32
    )
    attn_out = pieces_out.reshape(token_count, local_width).astype(jnp.bfloat16)
    middle = inputs + branch_total(product(attn_out, proj_weight))
    normed_two, normal_two, inverse_two = affine_norm(middle, ln2_gain, ln2_bias)
    mlp_in = normed_two.astype(jnp.bfloat16)
    mlp_pre = product(mlp_in, fc_in_weight)
    activated = jax.nn.gelu(mlp_pre, approximate=False).astype(jnp.bfloat16)
    hidden = middle + branch_total(product(activated, fc_out_weight))
    hidden_out = hidden.astype(jnp.bfloat16)
    masked_count = mask_index.shape[1]
    row_count = COPIES * masked_count
    hid_width = input_weight.shape[1]
    index_rows = mask_index[0]
    cond_in = hidden_out[index_rows]
    cond_pre = product(cond_in, cond_weight)
    time_flat = timesteps.reshape(row_count)
    embedded = frequency(time_flat).astype(jnp.bfloat16)
    time_pre = product(embedded, time_in_weight)
    time_act = jax.nn.silu(time_pre).astype(jnp.bfloat16)
    time_emb = product(time_act, time_out_weight)
    condition = (time_emb.reshape(COPIES, masked_count, HW) + cond_pre[None]).reshape(row_count, HW)
    cond_act = jax.nn.silu(condition).astype(jnp.bfloat16)
    abar_now, alpha_step, beta_step, beta_tilde, one_minus_now = plan(time_flat[:, None])
    start_rows = jnp.broadcast_to(targets, (COPIES,) + targets.shape).reshape(row_count, TOKCH)
    eps_true = noise.reshape(row_count, TOKCH)
    noisy_rows = (jnp.sqrt(abar_now) * start_rows + jnp.sqrt(one_minus_now) * eps_true).astype(
        jnp.bfloat16
    )
    residual = product(noisy_rows, input_weight)
    stored = []
    for layer_index in range(DEPTH):
        normal, inverse = sharded_norm(residual)
        modulation = product(cond_act, ada_weight[layer_index].reshape(HW, 3 * hid_width)).reshape(
            row_count, 3, hid_width
        )
        modulated = (normal * (1.0 + modulation[:, 1]) + modulation[:, 0]).astype(jnp.bfloat16)
        gathered = lax.all_gather(modulated, "tensor", axis=1, tiled=True)
        block_pre = product(gathered, block_in_weight[layer_index])
        block_act = jax.nn.silu(block_pre).astype(jnp.bfloat16)
        block_out = lax.psum_scatter(
            product(block_act, block_out_weight[layer_index]),
            "tensor",
            scatter_dimension=1,
            tiled=True,
        )
        stored.append((normal, inverse, modulation, gathered, block_pre, block_act, block_out))
        residual = residual + modulation[:, 2] * block_out
    final_normal, final_inverse = sharded_norm(residual)
    final_mod = product(cond_act, final_ada_weight.reshape(HW, 2 * hid_width)).reshape(
        row_count, 2, hid_width
    )
    final_in = (final_normal * (1.0 + final_mod[:, 1]) + final_mod[:, 0]).astype(jnp.bfloat16)
    predicted = lax.psum(product(final_in, out_weight), "tensor")
    coef_diff = beta_step / jnp.sqrt(one_minus_now * alpha_step)
    row_loss, loss_back = jax.vjp(
        lambda outputs: loss_rows(outputs, eps_true, beta_step, beta_tilde, coef_diff), predicted
    )
    loss_total = jnp.sum(row_loss)
    grad_pred = loss_back(jnp.full(row_loss.shape, 1.0 / COPIES, jnp.float32))[0].astype(
        jnp.bfloat16
    )
    out_weight_grad = product(final_in.T, grad_pred)
    grad_final_in = product(grad_pred, out_weight.T)
    grad_fmod = jnp.stack([grad_final_in, grad_final_in * final_normal], axis=1).astype(
        jnp.bfloat16
    )
    grad_fmod_flat = grad_fmod.reshape(row_count, 2 * hid_width)
    final_ada_grad = product(cond_act.T, grad_fmod_flat).reshape(HW, 2, hid_width)
    cond_partial = product(grad_fmod_flat, final_ada_weight.reshape(HW, 2 * hid_width).T)
    grad_resid = sharded_back(grad_final_in * (1.0 + final_mod[:, 1]), final_normal, final_inverse)
    ada_grads = [None] * DEPTH
    in_grads = [None] * DEPTH
    out_grads = [None] * DEPTH
    for layer_index in reversed(range(DEPTH)):
        normal, inverse, modulation, gathered, block_pre, block_act, block_out = stored[layer_index]
        grad_branch = (modulation[:, 2] * grad_resid).astype(jnp.bfloat16)
        grad_gate = grad_resid * block_out
        branch_full = lax.all_gather(grad_branch, "tensor", axis=1, tiled=True)
        out_grads[layer_index] = product(block_act.T, branch_full)
        grad_act = product(branch_full, block_out_weight[layer_index].T)
        grad_pre = jax.vjp(jax.nn.silu, block_pre)[1](grad_act)[0].astype(jnp.bfloat16)
        in_grads[layer_index] = product(gathered.T, grad_pre)
        grad_mod_in = lax.psum_scatter(
            product(grad_pre, block_in_weight[layer_index].T),
            "tensor",
            scatter_dimension=1,
            tiled=True,
        )
        grad_mod = jnp.stack([grad_mod_in, grad_mod_in * normal, grad_gate], axis=1).astype(
            jnp.bfloat16
        )
        grad_mod_flat = grad_mod.reshape(row_count, 3 * hid_width)
        ada_grads[layer_index] = product(cond_act.T, grad_mod_flat).reshape(HW, 3, hid_width)
        cond_partial = cond_partial + product(
            grad_mod_flat, ada_weight[layer_index].reshape(HW, 3 * hid_width).T
        )
        grad_resid = grad_resid + sharded_back(
            grad_mod_in * (1.0 + modulation[:, 1]), normal, inverse
        )
    ada_stack = jnp.stack(ada_grads)
    in_stack = jnp.stack(in_grads)
    out_stack = jnp.stack(out_grads)
    input_weight_grad = product(noisy_rows.T, grad_resid.astype(jnp.bfloat16))
    cond_grad_act = lax.psum(cond_partial, "tensor")
    grad_cond = jax.vjp(jax.nn.silu, condition)[1](cond_grad_act)[0]
    grad_time_emb = grad_cond.astype(jnp.bfloat16)
    time_out_grad = product(time_act.T, grad_time_emb)
    grad_time_act = product(grad_time_emb, time_out_weight.T)
    grad_time_pre = jax.vjp(jax.nn.silu, time_pre)[1](grad_time_act)[0].astype(jnp.bfloat16)
    time_in_grad = product(embedded.T, grad_time_pre)
    grad_cond_pre = jnp.sum(grad_cond.reshape(COPIES, masked_count, HW), axis=0).astype(
        jnp.bfloat16
    )
    cond_grad = product(cond_in.T, grad_cond_pre)
    grad_cond_in = product(grad_cond_pre, cond_weight.T)
    grad_hidden = (
        jnp.zeros((token_count, model_width), jnp.float32).at[index_rows].add(grad_cond_in)
    )
    grad_mlp = grad_hidden.astype(jnp.bfloat16)
    fc_out_grad = product(activated.T, grad_mlp)
    grad_act_mlp = product(grad_mlp, fc_out_weight.T)
    grad_mlp_pre = jax.vjp(partial(jax.nn.gelu, approximate=False), mlp_pre)[1](grad_act_mlp)[
        0
    ].astype(jnp.bfloat16)
    fc_in_grad = product(mlp_in.T, grad_mlp_pre)
    grad_normed_two = branch_total(product(grad_mlp_pre, fc_in_weight.T))
    grad_middle_part, ln2_gain_grad, ln2_bias_grad = affine_back(
        grad_normed_two, normal_two, inverse_two, ln2_gain
    )
    grad_middle = grad_hidden + grad_middle_part
    grad_attn = grad_middle.astype(jnp.bfloat16)
    proj_grad = product(attn_out.T, grad_attn)
    grad_attn_out = (
        product(grad_attn, proj_weight.T)
        .astype(jnp.bfloat16)
        .reshape(token_count, head_count, HEAD)
    )
    query_grads = []
    key_grad = jnp.zeros((token_count, head_count, HEAD), jnp.float32)
    value_grad = jnp.zeros((token_count, head_count, HEAD), jnp.float32)
    for index_block, start_row in enumerate(range(0, token_count, block_rows)):
        scores = block_scores(start_row)
        probability = jnp.exp(scores - log_totals[index_block])
        value_grad = jnp.einsum(
            "hqk,qhd->khd",
            probability.astype(jnp.bfloat16),
            grad_attn_out,
            preferred_element_type=jnp.float32,
        )
        grad_prob = jnp.einsum(
            "qhd,khd->hqk", grad_attn_out, value_rows, preferred_element_type=jnp.float32
        )
        row_delta = jnp.sum(probability * grad_prob, axis=-1, keepdims=True)
        grad_scores = (probability * (grad_prob - row_delta)).astype(jnp.bfloat16)
        query_grads.append(
            jnp.einsum("hqk,khd->qhd", grad_scores, key_rows, preferred_element_type=jnp.float32)
            * score_scale
        )
        key_grad = (
            jnp.einsum("hqk,qhd->khd", grad_scores, queries, preferred_element_type=jnp.float32)
            * score_scale
        )
    grad_qkv = jnp.concatenate(
        [
            query_grads[0].reshape(token_count, local_width),
            key_grad.reshape(token_count, local_width),
            value_grad.reshape(token_count, local_width),
        ],
        axis=1,
    ).astype(jnp.bfloat16)
    qkv_grad = product(attn_in.T, grad_qkv).reshape(model_width, 3, local_width)
    grad_normed_one = branch_total(product(grad_qkv, qkv_flat.T))
    grad_input_part, ln1_gain_grad, ln1_bias_grad = affine_back(
        grad_normed_one, normal_one, inverse_one, ln1_gain
    )
    input_grad = grad_middle + grad_input_part
    (
        qkv_red,
        proj_red,
        fc_in_red,
        fc_out_red,
        ada_red,
        in_red,
        out_red,
        final_red,
        cond_red,
        time_in_red,
        time_out_red,
    ) = (
        lax.psum_scatter(qkv_grad, "dp", scatter_dimension=0, tiled=True),
        lax.psum_scatter(proj_grad, "dp", scatter_dimension=1, tiled=True),
        lax.psum_scatter(fc_in_grad, "dp", scatter_dimension=0, tiled=True),
        lax.psum_scatter(fc_out_grad, "dp", scatter_dimension=1, tiled=True),
        lax.psum_scatter(ada_stack, "dp", scatter_dimension=1, tiled=True),
        lax.psum_scatter(in_stack, "dp", scatter_dimension=1, tiled=True),
        lax.psum_scatter(out_stack, "dp", scatter_dimension=2, tiled=True),
        lax.psum_scatter(final_ada_grad, "dp", scatter_dimension=0, tiled=True),
        lax.psum_scatter(cond_grad, "dp", scatter_dimension=0, tiled=True),
        lax.psum_scatter(time_in_grad, "dp", scatter_dimension=0, tiled=True),
        lax.psum_scatter(time_out_grad, "dp", scatter_dimension=0, tiled=True),
    )
    small_sums = lax.psum(
        (
            ln1_gain_grad,
            ln1_bias_grad,
            ln2_gain_grad,
            ln2_bias_grad,
            input_weight_grad,
            out_weight_grad,
            loss_total,
        ),
        "dp",
    )
    loss_mean = small_sums[6] / (lax.axis_size("dp") * row_count)
    return (
        loss_mean,
        hidden_out,
        input_grad,
        small_sums[0],
        small_sums[1],
        qkv_red,
        proj_red,
        small_sums[2],
        small_sums[3],
        fc_in_red,
        fc_out_red,
        cond_red,
        time_in_red,
        time_out_red,
        small_sums[4],
        ada_red,
        in_red,
        out_red,
        final_red,
        small_sums[5],
    )


def solution(mesh):
    placed = (
        P("dp", None),
        P("dp", None),
        P("dp", None),
        P("dp", None),
        P("dp", None, None),
        P(None, "dp", None, None),
        P(None, "dp", None),
        P(),
        P(),
        P(None, None, "tensor"),
        P("tensor", None),
        P(),
        P(),
        P(None, "tensor"),
        P("tensor", None),
        P(),
        P(),
        P(),
        P(None, "tensor"),
        P(None, None, None, "tensor"),
        P(None, None, "tensor"),
        P(None, "tensor", None),
        P(None, None, "tensor"),
        P("tensor", None),
    )
    return jax.shard_map(
        shards,
        mesh=mesh,
        in_specs=placed,
        out_specs=(
            P(),
            P("dp", None),
            P("dp", None),
            P(),
            P(),
            P("dp", None, "tensor"),
            P("tensor", "dp"),
            P(),
            P(),
            P("dp", "tensor"),
            P("tensor", "dp"),
            P("dp", None),
            P("dp", None),
            P("dp", None),
            P(None, "tensor"),
            P(None, "dp", None, "tensor"),
            P(None, "dp", "tensor"),
            P(None, "tensor", "dp"),
            P("dp", None, "tensor"),
            P("tensor", None),
        ),
        check_vma=False,
    )
```

profile of v0, /device:TPU:0, one launch (start us, length us, event | category | flops | bytes accessed | tf_op | source)
XLA Modules:
  0.0 3409.6 jit_solution(1101864485433149125)
XLA Ops:
  26.2 64.2 %all-reduce.24.cloned.1.call-done = f32[512,768]{1,0:T(8,128)} async-done(((f32[512,768]{1,0:T(8,128)}), f32[512,768]{1,0:T(8,128)}) %all-reduce.24.cloned.1.call-update) | async-done | bytes 1572880 | tf_op jit(solution)/shard_map/psum | solution.py:26
  193.9 54.0 %all-gather.13.cloned.1.call-done = bf16[1280,1024]{0,1:T(8,128)(2,1)} async-done(((bf16[1280,256]{0,1:T(8,128)(2,1)}), bf16[1280,1024]{0,1:T(8,128)(2,1)}) %all-gather.13.cloned.1.call-update) | async-done | bytes 2621456 | tf_op jit(solution)/shard_map/all_gather | solution.py:215
  265.9 82.9 %reduce-scatter.26.cloned.1.call-done = f32[1280,256]{0,1:T(8,128)} async-done(((f32[1280,1024]{0,1:T(8,128)}), f32[1280,256]{0,1:T(8,128)}) %reduce-scatter.26.cloned.1.call-update) | async-done | bytes 1310736 | tf_op jit(solution)/shard_map/reduce_scatter | solution.py:218
  373.1 53.3 %all-gather.15.cloned.1.call-done = bf16[1280,1024]{0,1:T(8,128)(2,1)} async-done(((bf16[1280,256]{0,1:T(8,128)(2,1)}), bf16[1280,1024]{0,1:T(8,128)(2,1)}) %all-gather.15.cloned.1.call-update) | async-done | bytes 2621456 | tf_op jit(solution)/shard_map/all_gather | solution.py:215
  443.3 83.3 %reduce-scatter.28.cloned.1.call-done = f32[1280,256]{0,1:T(8,128)} async-done(((f32[1280,1024]{0,1:T(8,128)}), f32[1280,256]{0,1:T(8,128)}) %reduce-scatter.28.cloned.1.call-update) | async-done | bytes 1310736 | tf_op jit(solution)/shard_map/reduce_scatter | solution.py:218
  550.8 53.3 %all-gather.17.cloned.1.call-done = bf16[1280,1024]{0,1:T(8,128)(2,1)} async-done(((bf16[1280,256]{0,1:T(8,128)(2,1)}), bf16[1280,1024]{0,1:T(8,128)(2,1)}) %all-gather.17.cloned.1.call-update) | async-done | bytes 2621456 | tf_op jit(solution)/shard_map/all_gather | solution.py:215
  621.8 83.2 %reduce-scatter.30.cloned.1.call-done = f32[1280,256]{0,1:T(8,128)} async-done(((f32[1280,1024]{0,1:T(8,128)}), f32[1280,256]{0,1:T(8,128)}) %reduce-scatter.30.cloned.1.call-update) | async-done | bytes 1310736 | tf_op jit(solution)/shard_map/reduce_scatter | solution.py:218
  729.6 53.3 %all-gather.19.cloned.1.call-done = bf16[1280,1024]{0,1:T(8,128)(2,1)} async-done(((bf16[1280,256]{0,1:T(8,128)(2,1)}), bf16[1280,1024]{0,1:T(8,128)(2,1)}) %all-gather.19.cloned.1.call-update) | async-done | bytes 2621456 | tf_op jit(solution)/shard_map/all_gather | solution.py:215
  800.2 83.5 %reduce-scatter.32.cloned.1.call-done = f32[1280,256]{0,1:T(8,128)} async-done(((f32[1280,1024]{0,1:T(8,128)}), f32[1280,256]{0,1:T(8,128)}) %reduce-scatter.32.cloned.1.call-update) | async-done | bytes 1310736 | tf_op jit(solution)/shard_map/reduce_scatter | solution.py:218
  908.4 53.3 %all-gather.21.cloned.1.call-done = bf16[1280,1024]{0,1:T(8,128)(2,1)} async-done(((bf16[1280,256]{0,1:T(8,128)(2,1)}), bf16[1280,1024]{0,1:T(8,128)(2,1)}) %all-gather.21.cloned.1.call-update) | async-done | bytes 2621456 | tf_op jit(solution)/shard_map/all_gather | solution.py:215
  979.4 83.3 %reduce-scatter.34.cloned.1.call-done = f32[1280,256]{0,1:T(8,128)} async-done(((f32[1280,1024]{0,1:T(8,128)}), f32[1280,256]{0,1:T(8,128)}) %reduce-scatter.34.cloned.1.call-update) | async-done | bytes 1310736 | tf_op jit(solution)/shard_map/reduce_scatter | solution.py:218
  1088.6 53.3 %all-gather.23.cloned.1.call-done = bf16[1280,1024]{0,1:T(8,128)(2,1)} async-done(((bf16[1280,256]{0,1:T(8,128)(2,1)}), bf16[1280,1024]{0,1:T(8,128)(2,1)}) %all-gather.23.cloned.1.call-update) | async-done | bytes 2621456 | tf_op jit(solution)/shard_map/all_gather | solution.py:215
  1160.5 82.3 %reduce-scatter.36.cloned.1.call-done = f32[1280,256]{0,1:T(8,128)} async-done(((f32[1280,1024]{0,1:T(8,128)}), f32[1280,256]{0,1:T(8,128)}) %reduce-scatter.36.cloned.1.call-update) | async-done | bytes 1310736 | tf_op jit(solution)/shard_map/reduce_scatter | solution.py:218
  1335.7 53.0 %all-gather.25.cloned.1.call-done = bf16[1280,1024]{0,1:T(8,128)(2,1)} async-done(((bf16[1280,256]{0,1:T(8,128)(2,1)}), bf16[1280,1024]{0,1:T(8,128)(2,1)}) %all-gather.25.cloned.1.call-update) | async-done | bytes 2621456 | tf_op jit(solution)/shard_map/all_gather | solution.py:256
  1397.2 92.6 %reduce-scatter.38.cloned.1.call-done = f32[1280,256]{0,1:T(8,128)} async-done(((f32[1280,1024]{0,1:T(8,128)}), f32[1280,256]{0,1:T(8,128)}) %reduce-scatter.38.cloned.1.call-update) | async-done | bytes 1310736 | tf_op jit(solution)/shard_map/reduce_scatter | solution.py:261
  1518.8 53.3 %all-gather.27.cloned.1.call-done = bf16[1280,1024]{0,1:T(8,128)(2,1)} async-done(((bf16[1280,256]{0,1:T(8,128)(2,1)}), bf16[1280,1024]{0,1:T(8,128)(2,1)}) %all-gather.27.cloned.1.call-update) | async-done | bytes 2621456 | tf_op jit(solution)/shard_map/all_gather | solution.py:256
  1580.6 92.6 %reduce-scatter.40.cloned.1.call-done = f32[1280,256]{0,1:T(8,128)} async-done(((f32[1280,1024]{0,1:T(8,128)}), f32[1280,256]{0,1:T(8,128)}) %reduce-scatter.40.cloned.1.call-update) | async-done | bytes 1310736 | tf_op jit(solution)/shard_map/reduce_scatter | solution.py:261
  1701.6 53.3 %all-gather.29.cloned.1.call-done = bf16[1280,1024]{0,1:T(8,128)(2,1)} async-done(((bf16[1280,256]{0,1:T(8,128)(2,1)}), bf16[1280,1024]{0,1:T(8,128)(2,1)}) %all-gather.29.cloned.1.call-update) | async-done | bytes 2621456 | tf_op jit(solution)/shard_map/all_gather | solution.py:256
  1763.5 92.6 %reduce-scatter.42.cloned.1.call-done = f32[1280,256]{0,1:T(8,128)} async-done(((f32[1280,1024]{0,1:T(8,128)}), f32[1280,256]{0,1:T(8,128)}) %reduce-scatter.42.cloned.1.call-update) | async-done | bytes 1310736 | tf_op jit(solution)/shard_map/reduce_scatter | solution.py:261
  1884.5 53.3 %all-gather.31.cloned.1.call-done = bf16[1280,1024]{0,1:T(8,128)(2,1)} async-done(((bf16[1280,256]{0,1:T(8,128)(2,1)}), bf16[1280,1024]{0,1:T(8,128)(2,1)}) %all-gather.31.cloned.1.call-update) | async-done | bytes 2621456 | tf_op jit(solution)/shard_map/all_gather | solution.py:256
  1946.3 92.6 %reduce-scatter.44.cloned.1.call-done = f32[1280,256]{0,1:T(8,128)} async-done(((f32[1280,1024]{0,1:T(8,128)}), f32[1280,256]{0,1:T(8,128)}) %reduce-scatter.44.cloned.1.call-update) | async-done | bytes 1310736 | tf_op jit(solution)/shard_map/reduce_scatter | solution.py:261
  2064.2 53.1 %all-gather.33.cloned.1.call-done = bf16[1280,1024]{0,1:T(8,128)(2,1)} async-done(((bf16[1280,256]{0,1:T(8,128)(2,1)}), bf16[1280,1024]{0,1:T(8,128)(2,1)}) %all-gather.33.cloned.1.call-update) | async-done | bytes 2621456 | tf_op jit(solution)/shard_map/all_gather | solution.py:256
  2125.9 92.6 %reduce-scatter.46.cloned.1.call-done = f32[1280,256]{0,1:T(8,128)} async-done(((f32[1280,1024]{0,1:T(8,128)}), f32[1280,256]{0,1:T(8,128)}) %reduce-scatter.46.cloned.1.call-update) | async-done | bytes 1310736 | tf_op jit(solution)/shard_map/reduce_scatter | solution.py:261
  2242.9 53.3 %all-gather.35.cloned.1.call-done = bf16[1280,1024]{0,1:T(8,128)(2,1)} async-done(((bf16[1280,256]{0,1:T(8,128)(2,1)}), bf16[1280,1024]{0,1:T(8,128)(2,1)}) %all-gather.35.cloned.1.call-update) | async-done | bytes 2621456 | tf_op jit(solution)/shard_map/all_gather | solution.py:256
  2344.8 52.5 %reduce-scatter.48.cloned.1.call-done = f32[1280,256]{0,1:T(8,128)} async-done(((f32[1280,1024]{0,1:T(8,128)}), f32[1280,256]{0,1:T(8,128)}) %reduce-scatter.48.cloned.1.call-update) | async-done | bytes 1310736 | tf_op jit(solution)/shard_map/reduce_scatter | solution.py:261
  2417.6 189.6 %all-reduce.30.cloned.1.call-done = f32[1280,1024]{1,0:T(8,128)} async-done(((f32[1280,1024]{1,0:T(8,128)}), f32[1280,1024]{1,0:T(8,128)}) %all-reduce.30.cloned.1.call-update) | async-done | bytes 5242896 | tf_op jit(solution)/shard_map/psum | solution.py:282
  2645.2 55.9 %all-reduce.32.cloned.1.call-done = f32[512,768]{1,0:T(8,128)} async-done(((f32[512,768]{1,0:T(8,128)}), f32[512,768]{1,0:T(8,128)}) %all-reduce.32.cloned.1.call-update) | async-done | bytes 1572880 | tf_op jit(solution)/shard_map/psum | solution.py:26
  2919.6 66.1 %reduce-scatter.64.cloned.1.call-done = f32[6,128,256]{2,1,0:T(8,128)} async-done(((f32[6,1024,256]{2,1,0:T(8,128)}), f32[6,128,256]{2,1,0:T(8,128)}) %reduce-scatter.64.cloned.1.call-update) | async-done | bytes 786448 | tf_op jit(solution)/shard_map/reduce_scatter | solution.py:373
  3071.8 46.6 %reduce-scatter.54.cloned.1.call-done = f32[768,96]{0,1:T(8,128)} async-done(((f32[768,768]{0,1:T(8,128)}), f32[768,96]{0,1:T(8,128)}) %reduce-scatter.54.cloned.1.call-update) | async-done | bytes 294928 | tf_op jit(solution)/shard_map/reduce_scatter | solution.py:371
  3164.9 50.5 %reduce-scatter.56.cloned.1.call-done = f32[96,1024]{1,0:T(8,128)} async-done(((f32[768,1024]{1,0:T(8,128)}), f32[96,1024]{1,0:T(8,128)}) %reduce-scatter.56.cloned.1.call-update) | async-done | bytes 393232 | tf_op jit(solution)/shard_map/reduce_scatter | solution.py:376
  3215.4 55.3 %reduce-scatter.60.cloned.1.call-done = f32[128,1024]{1,0:T(8,128)} async-done(((f32[1024,1024]{1,0:T(8,128)}), f32[128,1024]{1,0:T(8,128)}) %reduce-scatter.60.cloned.1.call-update) | async-done | bytes 524304 | tf_op jit(solution)/shard_map/reduce_scatter | solution.py:378
  3270.7 130.8 %reduce-scatter.62.cloned.1.call-done = f32[6,128,3,256]{3,1,2,0:T(8,128)} async-done(((f32[6,1024,3,256]{3,1,2,0:T(8,128)}), f32[6,128,3,256]{3,1,2,0:T(8,128)}) %reduce-scatter.62.cloned.1.call-update) | async-done | bytes 2359312 | tf_op jit(solution)/shard_map/reduce_scatter | solution.py:372
  (635 shorter events, 1078.5 us)
Async XLA Ops:
  193.8 154.9 %reduce-scatter.26.cloned.1.call-start = ((), (), s32[]{:S(2)}) async-start(), calls=%async_computation.26 | async-start | bytes 6553600 | tf_op jit(solution)/shard_map/reduce_scatter | solution.py:218
  256.1 170.3 %all-gather.15.cloned.1.call-start = ((), (), s32[]{:S(2)}) async-start(), calls=%async_computation.27 | async-start | bytes 3276800 | tf_op jit(solution)/shard_map/all_gather | solution.py:215
  433.9 170.2 %all-gather.17.cloned.1.call-start = ((), (), s32[]{:S(2)}) async-start(), calls=%async_computation.29 | async-start | bytes 3276800 | tf_op jit(solution)/shard_map/all_gather | solution.py:215
  550.7 154.2 %reduce-scatter.30.cloned.1.call-start = ((), (), s32[]{:S(2)}) async-start(), calls=%async_computation.30 | async-start | bytes 6553600 | tf_op jit(solution)/shard_map/reduce_scatter | solution.py:218
  612.3 170.6 %all-gather.19.cloned.1.call-start = ((), (), s32[]{:S(2)}) async-start(), calls=%async_computation.31 | async-start | bytes 3276800 | tf_op jit(solution)/shard_map/all_gather | solution.py:215
  791.1 170.6 %all-gather.21.cloned.1.call-start = ((), (), s32[]{:S(2)}) async-start(), calls=%async_computation.33 | async-start | bytes 3276800 | tf_op jit(solution)/shard_map/all_gather | solution.py:215
  908.4 154.3 %reduce-scatter.34.cloned.1.call-start = ((), (), s32[]{:S(2)}) async-start(), calls=%async_computation.34 | async-start | bytes 6553600 | tf_op jit(solution)/shard_map/reduce_scatter | solution.py:218
  970.0 172.0 %all-gather.23.cloned.1.call-start = ((), (), s32[]{:S(2)}) async-start(), calls=%async_computation.35 | async-start | bytes 3276800 | tf_op jit(solution)/shard_map/all_gather | solution.py:215
  1150.1 154.6 %all-reduce.28.cloned.1.call-start = ((), (), s32[]{:S(2)}) async-start(), calls=%async_computation.37 | async-start | bytes 327680 | tf_op jit(solution)/shard_map/psum | solution.py:231
  1397.2 174.9 %all-gather.27.cloned.1.call-start = ((), (), s32[]{:S(2)}) async-start(), calls=%async_computation.40 | async-start | bytes 3276800 | tf_op jit(solution)/shard_map/all_gather | solution.py:256
  1518.8 154.5 %reduce-scatter.40.cloned.1.call-start = ((), (), s32[]{:S(2)}) async-start(), calls=%async_computation.41 | async-start | bytes 6553600 | tf_op jit(solution)/shard_map/reduce_scatter | solution.py:261
  1580.5 174.4 %all-gather.29.cloned.1.call-start = ((), (), s32[]{:S(2)}) async-start(), calls=%async_computation.42 | async-start | bytes 3276800 | tf_op jit(solution)/shard_map/all_gather | solution.py:256
  1701.6 154.5 %reduce-scatter.42.cloned.1.call-start = ((), (), s32[]{:S(2)}) async-start(), calls=%async_computation.43 | async-start | bytes 6553600 | tf_op jit(solution)/shard_map/reduce_scatter | solution.py:261
  1763.4 174.4 %all-gather.31.cloned.1.call-start = ((), (), s32[]{:S(2)}) async-start(), calls=%async_computation.44 | async-start | bytes 3276800 | tf_op jit(solution)/shard_map/all_gather | solution.py:256
  1884.5 154.4 %reduce-scatter.44.cloned.1.call-start = ((), (), s32[]{:S(2)}) async-start(), calls=%async_computation.45 | async-start | bytes 6553600 | tf_op jit(solution)/shard_map/reduce_scatter | solution.py:261
  1946.2 171.1 %all-gather.33.cloned.1.call-start = ((), (), s32[]{:S(2)}) async-start(), calls=%async_computation.46 | async-start | bytes 3276800 | tf_op jit(solution)/shard_map/all_gather | solution.py:256
  2064.0 154.5 %reduce-scatter.46.cloned.1.call-start = ((), (), s32[]{:S(2)}) async-start(), calls=%async_computation.47 | async-start | bytes 6553600 | tf_op jit(solution)/shard_map/reduce_scatter | solution.py:261
  2125.8 170.4 %all-gather.35.cloned.1.call-start = ((), (), s32[]{:S(2)}) async-start(), calls=%async_computation.48 | async-start | bytes 3276800 | tf_op jit(solution)/shard_map/all_gather | solution.py:256
  2242.9 154.4 %reduce-scatter.48.cloned.1.call-start = ((), (), s32[]{:S(2)}) async-start(), calls=%async_computation.49 | async-start | bytes 6553600 | tf_op jit(solution)/shard_map/reduce_scatter | solution.py:261
  2304.7 302.5 %all-reduce.30.cloned.1.call-start = ((), (), s32[]{:S(2)}) async-start(), calls=%async_computation.50 | async-start | bytes 10485760 | tf_op jit(solution)/shard_map/psum | solution.py:282
  2417.5 283.6 %all-reduce.32.cloned.1.call-start = ((), (), s32[]{:S(2)}) async-start(), calls=%async_computation.51 | async-start | bytes 3145728 | tf_op jit(solution)/shard_map/psum | solution.py:26
  2632.9 183.7 %reduce-scatter.68.cloned.1.call-start = ((), (), s32[]{:S(2)}) async-start(), calls=%async_computation.62 | async-start | bytes 2359296 | tf_op jit(solution)/shard_map/reduce_scatter | solution.py:375
  2638.8 202.1 %reduce-scatter.70.cloned.1.call-start = ((), (), s32[]{:S(2)}) async-start(), calls=%async_computation.63 | async-start | bytes 884736
  2722.2 197.4 %reduce-scatter.66.cloned.1.call-start = ((), (), s32[]{:S(2)}) async-start(), calls=%async_computation.61 | async-start | bytes 7077888 | tf_op jit(solution)/shard_map/reduce_scatter | solution.py:374
  2733.4 252.3 %reduce-scatter.64.cloned.1.call-start = ((), (), s32[]{:S(2)}) async-start(), calls=%async_computation.60 | async-start | bytes 7077888 | tf_op jit(solution)/shard_map/reduce_scatter | solution.py:373
  2749.0 276.5 %reduce-scatter.58.cloned.1.call-start = ((), (), s32[]{:S(2)}) async-start(), calls=%async_computation.57 | async-start | bytes 1179648 | tf_op jit(solution)/shard_map/reduce_scatter | solution.py:377
  2758.8 313.0 %reduce-scatter.52.cloned.1.call-start = ((), (), s32[]{:S(2)}) async-start(), calls=%async_computation.54 | async-start | bytes 2654208 | tf_op jit(solution)/shard_map/reduce_scatter | solution.py:370
  2762.9 355.6 %reduce-scatter.54.cloned.1.call-start = ((), (), s32[]{:S(2)}) async-start(), calls=%async_computation.55 | async-start | bytes 2654208 | tf_op jit(solution)/shard_map/reduce_scatter | solution.py:371
  2766.8 398.0 %reduce-scatter.50.cloned.1.call-start = ((), (), s32[]{:S(2)}) async-start(), calls=%async_computation.53 | async-start | bytes 2654208 | tf_op jit(solution)/shard_map/reduce_scatter | solution.py:368
  2774.0 441.3 %reduce-scatter.56.cloned.1.call-start = ((), (), s32[]{:S(2)}) async-start(), calls=%async_computation.56 | async-start | bytes 3538944 | tf_op jit(solution)/shard_map/reduce_scatter | solution.py:376
  2778.1 492.6 %reduce-scatter.60.cloned.1.call-start = ((), (), s32[]{:S(2)}) async-start(), calls=%async_computation.58 | async-start | bytes 4718592 | tf_op jit(solution)/shard_map/reduce_scatter | solution.py:378
  2787.2 614.2 %reduce-scatter.62.cloned.1.call-start = ((), (), s32[]{:S(2)}) async-start(), calls=%async_computation.59 | async-start | bytes 21233664 | tf_op jit(solution)/shard_map/reduce_scatter | solution.py:372
  (166 other events, 2951.1 us)
Sparse Core Ops, SparseCore 0:
  18.5 71.7 all-reduce.23
  101.3 68.6 all-reduce.25
  194.0 53.8 all-gather.12
  256.2 92.5 reduce-scatter.25
  373.1 53.1 all-gather.14
  434.0 92.5 reduce-scatter.27
  550.8 53.2 all-gather.16
  612.4 92.5 reduce-scatter.29
  729.7 53.1 all-gather.18
  791.2 92.5 reduce-scatter.31
  908.5 53.1 all-gather.20
  970.1 92.5 reduce-scatter.33
  1088.7 53.1 all-gather.22
  1150.2 92.5 reduce-scatter.35
  1335.7 52.9 all-gather.24
  1397.3 92.5 reduce-scatter.37
  1518.9 53.1 all-gather.26
  1580.7 92.5 reduce-scatter.39
  1701.7 53.1 all-gather.28
  1763.5 92.5 reduce-scatter.41
  1884.6 53.1 all-gather.30
  1946.3 92.5 reduce-scatter.43
  2064.1 53.2 all-gather.32
  2126.0 92.5 reduce-scatter.45
  2243.0 53.1 all-gather.34
  2304.8 92.5 reduce-scatter.47
  2417.6 189.4 all-reduce.29
  2633.0 68.0 all-reduce.31
  2785.5 69.4 all-reduce.33
  2858.8 60.7 reduce-scatter.65
  2923.9 61.7 reduce-scatter.63
  3275.3 126.0 reduce-scatter.61
  (9 shorter events, 368.8 us)
where the time goes:
time: 3420 us; the launch traced here: 3410 us
  waiting for transfers between devices  2560 us (75%)
  matrix products  328 us (10%)
  blocking collectives  278 us (8%)
  other arithmetic  140 us (4%)
  local copies, waits for them, and re-layouts  78.6 us (2%)
    reduce_scatter x6, waiting for transfers between devices, shards(): lax.psum_scatter(product(grad_pre, block_in_weight[layer_index].T), 'tens...  516 us
    reduce_scatter x6, waiting for transfers between devices, shards(): lax.psum_scatter(product(block_act, block_out_weight[layer_index]), 'tens...  498 us
    all_gather x6, waiting for transfers between devices, shards(): gathered = lax.all_gather(modulated, 'tensor', axis=1, tiled=True)  320 us
    all_gather x6, waiting for transfers between devices, shards(): branch_full = lax.all_gather(grad_branch, 'tensor', axis=1, tiled=True)  319 us
    dot_general x80, matrix products, product(): return jnp.dot(left_op, right_op, preferred_element_type=jnp.float32)  317 us
    psum x14, blocking collectives, row_sums(): return lax.psum((first_sum, second_sum), 'tensor')  253 us
    psum x1, waiting for transfers between devices, shards(): cond_grad_act = lax.psum(cond_partial, 'tensor')  190 us
    psum x4, waiting for transfers between devices, branch_total(): return lax.psum(partial_sums, 'tensor')  171 us
  transfers between devices with their start and end apart: 41, of which 39 were waited for; matrix products, arithmetic and copies ran while one was open for 7% of the time, Pallas kernels for 0%

commit v1 on v0

v1 whole, which is shorter than its diff:
```python
from functools import partial
import math

import jax
import jax.numpy as jnp
from jax import lax
from jax.experimental import pallas as pl
from jax.experimental.pallas import tpu as pltpu
from jax.sharding import PartitionSpec as P

HEAD = 64
HW = 1024
DEPTH = 6
TOKCH = 16
FREQ = 256
COPIES = 4
STEPS = 1000

norm_eps = 1e-06
bf16 = jnp.bfloat16
f32 = jnp.float32


def product(left_op, right_op):
    return jnp.dot(left_op, right_op, preferred_element_type=f32)


def product_nt(left_op, right_op):
    return lax.dot_general(left_op, right_op, (((1,), (1,)), ((), ())), preferred_element_type=f32)


def product_tn(left_op, right_op):
    return lax.dot_general(left_op, right_op, (((0,), (0,)), ((), ())), preferred_element_type=f32)


def bit_list(size):
    bits = []
    while (1 << len(bits)) < size:
        bits.append(1 << len(bits))
    return bits


def flip(values, axis, mask):
    size = lax.axis_size(axis)
    return lax.ppermute(values, axis, [(i, i ^ mask) for i in range(size)])


def relabel(values, dim, count, own):
    step = values.shape[dim] // count
    return jnp.concatenate(
        [lax.dynamic_slice_in_dim(values, (own ^ r) * step, step, dim) for r in range(count)],
        axis=dim,
    )


def plain_norm(values):
    centred = values - jnp.mean(values, axis=-1, keepdims=True)
    inverse = lax.rsqrt(jnp.mean(centred * centred, axis=-1, keepdims=True) + norm_eps)
    return centred * inverse, inverse


def norm_back(grad_normal, normal, inverse):
    return inverse * (
        grad_normal
        - jnp.mean(grad_normal, axis=-1, keepdims=True)
        - normal * jnp.mean(grad_normal * normal, axis=-1, keepdims=True)
    )


def plan(time_rows):
    moment = time_rows.astype(f32)
    quarter = math.pi / 2.0
    angle_zero = 0.008 / 1.008 * quarter
    angle_now = ((moment + 1.0) / STEPS + 0.008) / 1.008 * quarter
    angle_prev = (moment / STEPS + 0.008) / 1.008 * quarter
    start_level = math.cos(angle_zero) ** 2
    abar_now = jnp.cos(angle_now) ** 2 / start_level
    abar_prev = jnp.cos(angle_prev) ** 2 / start_level
    one_minus_now = jnp.sin(angle_now - angle_zero) * jnp.sin(angle_now + angle_zero) / start_level
    one_minus_prev = (
        jnp.sin(angle_prev - angle_zero) * jnp.sin(angle_prev + angle_zero) / start_level
    )
    beta_step = (
        jnp.sin(angle_now - angle_prev) * jnp.sin(angle_now + angle_prev) / jnp.cos(angle_prev) ** 2
    )
    alpha_step = abar_now / abar_prev
    beta_tilde = beta_step * one_minus_prev / one_minus_now
    return (abar_now, alpha_step, beta_step, beta_tilde, one_minus_now)


def frequency(time_rows):
    half_width = FREQ // 2
    freq_rates = jnp.exp(-math.log(10000.0) * jnp.arange(half_width).astype(f32) / half_width)
    angles = time_rows.astype(f32)[:, None] * freq_rates[None, :]
    return jnp.concatenate([jnp.cos(angles), jnp.sin(angles)], axis=-1)


def loss_rows(predicted, eps_true, beta_step, beta_tilde, coef_diff):
    eps_pred = predicted[:, :TOKCH]
    var_raw = predicted[:, TOKCH:]
    squared = jnp.mean((eps_true - eps_pred) ** 2, axis=-1)
    fraction = (var_raw + 1.0) / 2.0
    log_tilde = jnp.log(beta_tilde)
    log_model = fraction * jnp.log(beta_step) + (1.0 - fraction) * log_tilde
    mean_gap = coef_diff * (eps_pred - eps_true)
    diverge = 0.5 * (
        -1.0
        + log_model
        - log_tilde
        + jnp.exp(log_tilde - log_model)
        + mean_gap * mean_gap * jnp.exp(-log_model)
    )
    return squared + jnp.mean(diverge, axis=-1) / math.log(2.0)


def gather_blocks(block):
    return [block] + [flip(block, "tensor", r) for r in range(1, lax.axis_size("tensor"))]


def scatter_sum(pieces):
    total = pieces[0].astype(f32)
    for r in range(1, len(pieces)):
        total = total + flip(pieces[r].astype(bf16), "tensor", r).astype(f32)
    return total


def gather_pack(chunk):
    full = lax.all_gather(chunk, ("dp", "tensor"), axis=0, tiled=False)
    return full.reshape((lax.axis_size("dp"), lax.axis_size("tensor")) + chunk.shape)


def reduce_pack(grads, z):
    part = lax.psum_scatter(grads, "dp", scatter_dimension=0, tiled=True)[0]
    return scatter_sum(
        [
            lax.dynamic_index_in_dim(part, z ^ r, axis=0, keepdims=False)
            for r in range(grads.shape[1])
        ]
    )


def reduce_outer(alive, order):
    for bit in order:
        going = sorted(k for k in alive if k & bit)
        sent = flip(jnp.stack([alive[k].astype(bf16) for k in going]), "dp", bit)
        alive = {
            k: alive[k] + sent[going.index(k | bit)].astype(f32) for k in alive if not k & bit
        }
    return alive[0]


def reduce_dp(keep, send):
    outer = bit_list(lax.axis_size("dp"))[1:]
    total = keep.astype(f32) + flip(send.astype(bf16), "dp", 1).astype(f32)
    return reduce_outer({2 * k: total[k] for k in range(total.shape[0])}, outer)


def reduce_halves(keep, send):
    outer = bit_list(lax.axis_size("dp"))[1:]
    total = keep.astype(f32) + flip(send, "dp", 1).astype(f32)
    half = keep.shape[1] // 2
    chunks = range(keep.shape[0])
    low = reduce_outer({2 * k: total[k, :half] for k in chunks}, outer)
    high = reduce_outer({2 * k: total[k, half:] for k in chunks}, outer[::-1])
    return scatter_sum([low[r] for r in range(half)] + [high[r] for r in range(half)])


VMEM_LIMIT = 60 * 1024 * 1024


def silu_pair(x):
    sig = 1.0 / (1.0 + jnp.exp(-x))
    return x * sig, sig * (1.0 + x * (1.0 - sig))


def weight(ref):
    n, _, _, c, w = ref.shape
    return ref[...].reshape(n * c, w)


def forward_kernel(
    resid_ref, cond_ref, a0_ref, a1_ref, a2_ref, in_ref, outw_ref,
    scale_ref, gate_ref, pre_ref, mod_ref, out_ref, next_ref, normal_s,
):
    s = pl.program_id(0)
    t = pl.num_programs(0) // 2
    hid = pre_ref.shape[1]

    @pl.when(s == 0)
    def _():
        normal_s[...] = plain_norm(resid_ref[...])[0]
        out_ref[...] = jnp.zeros_like(out_ref)

    @pl.when(s < t)
    def _():
        cond = cond_ref[...]
        cols = pl.ds(pl.multiple_of(s * hid, hid), hid)
        shift = product(cond, weight(a0_ref))
        scale = product(cond, weight(a1_ref))
        scale_ref[...] = scale
        gate_ref[:, cols] = product(cond, weight(a2_ref))
        mod_ref[:, cols] = (normal_s[:, cols] * (1.0 + scale) + shift).astype(bf16)

    @pl.when(s >= t)
    def _():
        pre = product(mod_ref[...], weight(in_ref))
        pre_ref[...] = pre
        out_ref[...] += product_nt(silu_pair(pre)[0].astype(bf16), weight(outw_ref))

    @pl.when(s == 2 * t - 1)
    def _():
        next_ref[...] = resid_ref[...] + gate_ref[...] * out_ref[...]


def whole(shape, dtype=None):
    return pl.BlockSpec(shape, lambda s: (0,) * len(shape), pipeline_mode=pl.Buffered(1))


def out_whole(shape):
    return pl.BlockSpec(shape, lambda s: (0,) * len(shape))


def params():
    return pltpu.CompilerParams(vmem_limit_bytes=VMEM_LIMIT)


def cost(flops, nbytes):
    return pl.CostEstimate(flops=int(flops), bytes_accessed=int(nbytes), transcendentals=0)


def pack_spec(pack, column, block):
    n, _, _, c, w = pack.shape
    return pl.BlockSpec((n, 1, 1, c, w), lambda s: (0, block(s), column, 0, 0))


def layer_forward(resid, cond, pack, first):
    rows = resid.shape[0]
    n, t, _, c, hid = pack.shape
    early = lambda s: jnp.minimum(s, t - 1)
    late = lambda s: jnp.maximum(s - t, 0)
    full = jax.ShapeDtypeStruct((rows, HW), f32)
    return pl.pallas_call(
        forward_kernel,
        grid=(2 * t,),
        in_specs=[whole((rows, HW)), whole((rows, HW))]
        + [pack_spec(pack, first + k, early) for k in range(3)]
        + [pack_spec(pack, first + k, late) for k in (3, 4)],
        out_specs=[
            pl.BlockSpec((rows, hid), lambda s: (0, early(s))),
            out_whole((rows, HW)),
            pl.BlockSpec((rows, hid), lambda s: (0, late(s))),
            out_whole((rows, HW)),
            out_whole((rows, HW)),
            out_whole((rows, HW)),
        ],
        out_shape=[full, full, full, jax.ShapeDtypeStruct((rows, HW), bf16), full, full],
        scratch_shapes=[pltpu.VMEM((rows, HW), f32)],
        compiler_params=params(),
        cost_estimate=cost(2 * rows * HW * 5 * HW, 10 * HW * HW + 30 * rows * HW),
    )(resid, cond, *[pack] * 5)


def backward_kernel(
    where_ref, gres_ref, resid_ref, scale_ref, gate_ref, out_ref, cond_ref, mod_ref, gc_ref, pre_ref,
    a0_ref, a1_ref, a2_ref, in_ref, outw_ref, *rest, split,
):
    if split:
        gnext_ref, gcn_ref, keep_ref, send_ref, normal_s, branch_s, gmi_s, dio_s = rest
        grad_ref = keep_ref
    else:
        gnext_ref, gcn_ref, grad_ref, normal_s, branch_s, gmi_s, dio_s = rest[-7:]
    s = pl.program_id(0)
    t = pl.num_programs(0) // 2
    hid = pre_ref.shape[1]
    d = where_ref[0]

    def put(k, value):
        c = grad_ref.shape[3]
        if not split:
            grad_ref[:, 0, k] = value.reshape(grad_ref.shape[0], c, hid)
            return
        value = value.reshape(2 * keep_ref.shape[0], c, hid)
        for parity in range(2):

            @pl.when((d & 1) == parity)
            def _():
                for chunk in range(value.shape[0]):
                    ref = keep_ref if (chunk & 1) == parity else send_ref
                    ref[(d ^ chunk) >> 1, 0, k] = value[chunk]

    @pl.when(s == 0)
    def _():
        branch_s[...] = (gate_ref[...] * gres_ref[...]).astype(bf16)
        gmi_s[...] = jnp.zeros_like(gmi_s)
        gcn_ref[...] = gc_ref[...]

    @pl.when(s < t)
    def _():
        grad_act = product(branch_s[...], weight(outw_ref))
        act, slope = silu_pair(pre_ref[...])
        grad_pre = (grad_act * slope).astype(bf16)
        gmi_s[...] += product_nt(grad_pre, weight(in_ref))
        dio_s[s, 0] = product_tn(mod_ref[...], grad_pre).astype(bf16)
        dio_s[s, 1] = product_tn(branch_s[...], act.astype(bf16)).astype(bf16)

    @pl.when(s == t - 1)
    def _():
        normal, inverse = plain_norm(resid_ref[...])
        normal_s[...] = normal
        gnext_ref[...] = gres_ref[...] + norm_back(
            gmi_s[...] * (1.0 + scale_ref[...]), normal, inverse
        )

    @pl.when(s >= t)
    def _():
        cols = pl.ds(pl.multiple_of((s - t) * hid, hid), hid)
        grad_mod_in = gmi_s[:, cols]
        grad_mods = (
            grad_mod_in.astype(bf16),
            (grad_mod_in * normal_s[:, cols]).astype(bf16),
            (gres_ref[:, cols] * out_ref[:, cols]).astype(bf16),
        )
        back = None
        for k, ref in enumerate((a0_ref, a1_ref, a2_ref)):
            put(k, product_tn(cond_ref[...], grad_mods[k]).astype(bf16))
            term = product_nt(grad_mods[k], weight(ref))
            back = term if back is None else back + term
        gcn_ref[...] += back
        for k in range(2):
            put(3 + k, dio_s[s - t, k])


def layer_backward(where, grad_resid, saved, cond, grad_cond, pack, first, grads, place, count):
    resid, scale, gate, pre, mod, out = saved
    rows = resid.shape[0]
    n, t, _, c, hid = pack.shape
    split = count == 0
    early = lambda s: jnp.minimum(s, t - 1)
    late = lambda s: jnp.maximum(s - t, 0)
    full = jax.ShapeDtypeStruct((rows, HW), f32)
    held = [] if grads is None else [grads]

    def resident(shape, **kw):
        return pl.BlockSpec(shape, lambda s, where: (0,) * len(shape), **kw)

    def weights(k, block):
        return pl.BlockSpec((n, 1, 1, c, hid), lambda s, where: (0, block(s), first + k, 0, 0))

    if split:
        pack_out = [
            pl.BlockSpec((n // 2, 1, 5, c, hid), lambda s, where: (0, late(s) ^ where[1], 0, 0, 0))
        ] * 2
        pack_shape = [jax.ShapeDtypeStruct((n // 2, t, 5, c, hid), bf16)] * 2
    else:
        pack_out = [
            pl.BlockSpec((n, 1, 5, c, hid), lambda s, where: (0, late(s), place, 0, 0))
        ]
        pack_shape = [jax.ShapeDtypeStruct((n, t, 5 * count, c, hid), bf16)]
    return pl.pallas_call(
        partial(backward_kernel, split=split),
        grid_spec=pltpu.PrefetchScalarGridSpec(
            num_scalar_prefetch=1,
            grid=(2 * t,),
            in_specs=[resident((rows, HW), pipeline_mode=pl.Buffered(1))] * 8
            + [pl.BlockSpec((rows, hid), lambda s, where: (0, early(s)))]
            + [weights(k, late) for k in range(3)]
            + [weights(k, early) for k in (3, 4)]
            + [pl.BlockSpec(memory_space=pl.ANY)] * len(held),
            out_specs=[resident((rows, HW)), resident((rows, HW))] + pack_out,
            scratch_shapes=[
                pltpu.VMEM((rows, HW), f32),
                pltpu.VMEM((rows, HW), bf16),
                pltpu.VMEM((rows, HW), f32),
                pltpu.VMEM((t, 2, HW, hid), bf16),
            ],
        ),
        out_shape=[full, full] + pack_shape,
        input_output_aliases={15: 2} if held else {},
        compiler_params=params(),
        cost_estimate=cost(4 * rows * HW * 5 * HW, 20 * HW * HW + 40 * rows * HW),
    )(where, grad_resid, resid, scale, gate, out, cond, mod, grad_cond, pre, *[pack] * 5, *held)


def final_kernel(
    resid_ref, cond_ref, eps_ref, coef_ref, wm_ref, wv_ref, f0_ref, f1_ref,
    gres_ref, gc_ref, grad_ref, loss_ref, dm_ref, dv_ref,
    scale_s, shift_s, normal_s, gfin_s,
):
    s = pl.program_id(0)
    t = pl.num_programs(0) // 2
    hid = f0_ref.shape[4]
    piece = (grad_ref.shape[0], grad_ref.shape[3], hid)

    @pl.when(s < t)
    def _():
        cols = pl.ds(pl.multiple_of(s * hid, hid), hid)
        shift_s[:, cols] = product(cond_ref[...], weight(f0_ref))
        scale_s[:, cols] = 1.0 + product(cond_ref[...], weight(f1_ref))

    @pl.when(s == t - 1)
    def _():
        normal, inverse = plain_norm(resid_ref[...])
        normal_s[...] = normal
        final_in = (normal * scale_s[...] + shift_s[...]).astype(bf16)
        eps_pred = product(final_in, wm_ref[...])
        var_raw = product(final_in, wv_ref[...])
        log_beta, log_tilde, coef = coef_ref[:, 0:1], coef_ref[:, 1:2], coef_ref[:, 2:3]
        miss = eps_pred - eps_ref[...]
        fraction = (var_raw + 1.0) / 2.0
        log_model = fraction * log_beta + (1.0 - fraction) * log_tilde
        mean_gap = coef * miss
        ratio = jnp.exp(log_tilde - log_model)
        precision = jnp.exp(-log_model)
        diverge = 0.5 * (
            -1.0 + log_model - log_tilde + ratio + mean_gap * mean_gap * precision
        )
        row_loss = jnp.mean(miss * miss, axis=-1, keepdims=True) + jnp.mean(
            diverge, axis=-1, keepdims=True
        ) / math.log(2.0)
        loss_ref[...] = jnp.broadcast_to(jnp.sum(row_loss, axis=0, keepdims=True), loss_ref.shape)
        share = 1.0 / (COPIES * TOKCH)
        grad_miss = (
            share * (2.0 * miss + mean_gap * precision * coef / math.log(2.0))
        ).astype(bf16)
        grad_var = (
            (share * 0.25 / math.log(2.0))
            * (1.0 - ratio - mean_gap * mean_gap * precision)
            * (log_beta - log_tilde)
        ).astype(bf16)
        dm_ref[...] = product_tn(final_in, grad_miss)
        dv_ref[...] = product_tn(final_in, grad_var)
        grad_fin = product_nt(grad_miss, wm_ref[...]) + product_nt(grad_var, wv_ref[...])
        gfin_s[...] = grad_fin
        gres_ref[...] = norm_back(grad_fin * scale_s[...], normal, inverse)
        gc_ref[...] = jnp.zeros_like(gc_ref)

    @pl.when(s >= t)
    def _():
        cols = pl.ds(pl.multiple_of((s - t) * hid, hid), hid)
        grad_fin = gfin_s[:, cols]
        grad_mods = (grad_fin.astype(bf16), (grad_fin * normal_s[:, cols]).astype(bf16))
        for k, ref in enumerate((f0_ref, f1_ref)):
            grad_ref[:, 0, k] = (
                product_tn(cond_ref[...], grad_mods[k]).astype(bf16).reshape(piece)
            )
            gc_ref[...] += product_nt(grad_mods[k], weight(ref))


def final_layer(resid, cond, eps_true, coefs, w_mean, w_var, pack, first):
    rows = resid.shape[0]
    n, t, _, c, hid = pack.shape
    full = jax.ShapeDtypeStruct((rows, HW), f32)
    thin = jax.ShapeDtypeStruct((HW, TOKCH), f32)
    both = lambda s: jnp.where(s < t, s, s - t)
    late = lambda s: jnp.maximum(s - t, 0)
    return pl.pallas_call(
        final_kernel,
        grid=(2 * t,),
        in_specs=[
            whole((rows, HW)),
            whole((rows, HW)),
            whole((rows, TOKCH)),
            whole((rows, 4)),
            whole((HW, TOKCH)),
            whole((HW, TOKCH)),
        ]
        + [pack_spec(pack, first + k, both) for k in range(2)],
        out_specs=[
            out_whole((rows, HW)),
            out_whole((rows, HW)),
            pl.BlockSpec((n, 1, 2, c, hid), lambda s: (0, late(s), 0, 0, 0)),
            out_whole((8, 128)),
            out_whole((HW, TOKCH)),
            out_whole((HW, TOKCH)),
        ],
        out_shape=[
            full,
            full,
            jax.ShapeDtypeStruct((n, t, 2, c, hid), bf16),
            jax.ShapeDtypeStruct((8, 128), f32),
            thin,
            thin,
        ],
        scratch_shapes=[pltpu.VMEM((rows, HW), f32)] * 4,
        compiler_params=params(),
        cost_estimate=cost(6 * rows * HW * 2 * HW, 8 * HW * HW + 20 * rows * HW),
    )(resid, cond, eps_true, coefs, w_mean, w_var, pack, pack)


def condition_kernel(
    emb_ref, in_ref, wti_ref, wto_ref, wc_ref, tpre_ref, tact_ref, condition_ref, cond_ref
):
    time_pre = product(emb_ref[...], wti_ref[...])
    tpre_ref[...] = time_pre
    time_act = silu_pair(time_pre)[0].astype(bf16)
    tact_ref[...] = time_act
    time_emb = product(time_act, wto_ref[...])
    cond_pre = product(in_ref[...], wc_ref[...])
    masked = in_ref.shape[0]
    for c in range(COPIES):
        rows = slice(c * masked, (c + 1) * masked)
        condition_ref[rows, :] = time_emb[rows] + cond_pre
    cond_ref[...] = silu_pair(condition_ref[...])[0].astype(bf16)


def vmem_spec():
    return pl.BlockSpec(memory_space=pltpu.VMEM)


def condition_forward(embedded, cond_in, time_in_weight, time_out_weight, cond_weight):
    rows = embedded.shape[0]
    full = jax.ShapeDtypeStruct((rows, HW), f32)
    low = jax.ShapeDtypeStruct((rows, HW), bf16)
    return pl.pallas_call(
        condition_kernel,
        in_specs=[vmem_spec()] * 5,
        out_specs=[vmem_spec()] * 4,
        out_shape=[full, low, full, low],
        compiler_params=params(),
        cost_estimate=cost(2 * rows * HW * 2 * HW, 4 * HW * HW + 10 * rows * HW),
    )(embedded, cond_in, time_in_weight, time_out_weight, cond_weight)


def condition_back_kernel(
    gc_ref, condition_ref, tpre_ref, tact_ref, emb_ref, in_ref, wto_ref, wc_ref,
    gin_ref, dto_ref, dti_ref, dc_ref, gcond_s,
):
    gcond_s[...] = gc_ref[...] * silu_pair(condition_ref[...])[1]
    grad_temb = gcond_s[...].astype(bf16)
    masked = in_ref.shape[0]
    total = gcond_s[0:masked, :]
    for c in range(1, COPIES):
        total = total + gcond_s[c * masked : (c + 1) * masked, :]
    grad_cpre = total.astype(bf16)
    gin_ref[...] = product_nt(grad_cpre, wc_ref[...]).astype(bf16)
    dc_ref[...] = product_tn(in_ref[...], grad_cpre).astype(bf16)
    grad_tact = product_nt(grad_temb, wto_ref[...])
    dto_ref[...] = product_tn(tact_ref[...], grad_temb).astype(bf16)
    grad_tpre = (grad_tact * silu_pair(tpre_ref[...])[1]).astype(bf16)
    dti_ref[...] = product_tn(emb_ref[...], grad_tpre).astype(bf16)


def condition_backward(
    grad_cond, condition, time_pre, time_act, embedded, cond_in, time_out_weight, cond_weight
):
    rows = embedded.shape[0]
    return pl.pallas_call(
        condition_back_kernel,
        in_specs=[vmem_spec()] * 8,
        out_specs=[vmem_spec()] * 4,
        out_shape=[
            jax.ShapeDtypeStruct(cond_in.shape, bf16),
            jax.ShapeDtypeStruct((HW, HW), bf16),
            jax.ShapeDtypeStruct((embedded.shape[1], HW), bf16),
            jax.ShapeDtypeStruct((cond_in.shape[1], HW), bf16),
        ],
        scratch_shapes=[pltpu.VMEM((rows, HW), f32)],
        compiler_params=params(),
        cost_estimate=cost(4 * rows * HW * 2 * HW, 10 * HW * HW + 20 * rows * HW),
    )(
        grad_cond, condition, time_pre, time_act, embedded, cond_in, time_out_weight,
        cond_weight,
    )


def butterfly(values, axis):
    for bit in bit_list(lax.axis_size(axis)):
        values = values + flip(values, axis, bit)
    return values


def shards(
    tokens,
    segment_ids,
    visible,
    mask_index,
    targets,
    noise,
    timesteps,
    ln1_gain,
    ln1_bias,
    qkv_weight,
    proj_weight,
    ln2_gain,
    ln2_bias,
    fc_in_weight,
    fc_out_weight,
    cond_weight,
    time_in_weight,
    time_out_weight,
    input_weight,
    ada_weight,
    block_in_weight,
    block_out_weight,
    final_ada_weight,
    out_weight,
):
    t, z = lax.axis_size("tensor"), lax.axis_index("tensor")
    n, d = lax.axis_size("dp"), lax.axis_index("dp")
    token_count, model_width = tokens.shape
    local_width = qkv_weight.shape[2]
    head_count = local_width // HEAD
    hid = input_weight.shape[1]
    chunk_rows = HW // n
    score_scale = 1.0 / math.sqrt(HEAD)
    own_rows = token_count // t

    ada_chunk = lax.dynamic_slice_in_dim(ada_weight, d * chunk_rows, chunk_rows, 1)
    in_chunk = lax.dynamic_slice_in_dim(block_in_weight, d * chunk_rows, chunk_rows, 1)
    out_chunk = lax.dynamic_slice_in_dim(block_out_weight, d * chunk_rows, chunk_rows, 2)
    def layer_chunk(l):
        return [
            jnp.moveaxis(ada_chunk[l], 1, 0),
            in_chunk[l][None],
            out_chunk[l].T[None],
        ]

    final_chunk = lax.dynamic_slice_in_dim(final_ada_weight, d * chunk_rows, chunk_rows, 0)
    half_depth = DEPTH // 2
    first_pack = gather_pack(
        jnp.concatenate(sum([layer_chunk(l) for l in range(half_depth)], []), axis=0)
    )
    second_pack = gather_pack(
        jnp.concatenate(
            sum([layer_chunk(l) for l in range(half_depth, DEPTH)], [])
            + [jnp.moveaxis(final_chunk, 1, 0)],
            axis=0,
        )
    )

    def pack_of(l):
        return (first_pack, 5 * l) if l < half_depth else (second_pack, 5 * (l - half_depth))

    input_full = relabel(jnp.concatenate(gather_blocks(input_weight), axis=1), 1, t, z)
    out_full = relabel(jnp.concatenate(gather_blocks(out_weight), axis=0), 0, t, z)

    inputs = relabel(tokens, 0, t, z).astype(f32)
    segments = relabel(segment_ids[0], 0, t, z)
    shown_keys = relabel(visible[0], 0, t, z)
    normal_one, inverse_one = plain_norm(inputs)
    attn_in = (normal_one * ln1_gain + ln1_bias).astype(bf16)
    qkv_flat = qkv_weight.reshape(model_width, 3 * local_width)
    projected = product(attn_in, qkv_flat).astype(bf16)
    queries = projected[:, :local_width].reshape(token_count, head_count, HEAD)
    key_rows = projected[:, local_width : 2 * local_width].reshape(token_count, head_count, HEAD)
    value_rows = projected[:, 2 * local_width :].reshape(token_count, head_count, HEAD)
    positions = jnp.arange(token_count)
    allowed = (segments[:, None] == segments[None, :]) & (
        (shown_keys[None, :] == 1) | (positions[:, None] == positions[None, :])
    )
    scores = (
        jnp.einsum("qhd,khd->hqk", queries, key_rows, preferred_element_type=f32) * score_scale
    )
    scores = jnp.where(allowed[None], scores, -1e30)
    row_top = jnp.max(scores, axis=-1, keepdims=True)
    weights_exp = jnp.exp(scores - row_top)
    row_total = jnp.sum(weights_exp, axis=-1, keepdims=True)
    probability = weights_exp / row_total
    prob_low = probability.astype(bf16)
    attn_out = (
        jnp.einsum("hqk,khd->qhd", prob_low, value_rows, preferred_element_type=f32)
        .reshape(token_count, local_width)
        .astype(bf16)
    )

    def row_blocks(values):
        return [values[r * own_rows : (r + 1) * own_rows] for r in range(t)]

    middle = inputs[:own_rows] + scatter_sum(row_blocks(product(attn_out, proj_weight)))
    normal_two, inverse_two = plain_norm(middle)
    mlp_in = jnp.concatenate(
        gather_blocks((normal_two * ln2_gain + ln2_bias).astype(bf16)), axis=0
    )
    mlp_pre = product(mlp_in, fc_in_weight)
    activated = jax.nn.gelu(mlp_pre, approximate=False).astype(bf16)
    hidden = middle + scatter_sum(row_blocks(product(activated, fc_out_weight)))
    hidden_rel = jnp.concatenate(gather_blocks(hidden.astype(bf16)), axis=0)
    hidden_out = relabel(hidden_rel, 0, t, z)

    masked_count = mask_index.shape[1]
    own_masked = masked_count // t
    row_count = COPIES * own_masked
    index_all = mask_index[0]
    index_all = ((index_all // own_rows) ^ z) * own_rows + index_all % own_rows
    index_all = relabel(index_all, 0, t, z)
    cond_in = hidden_rel[index_all[:own_masked]]
    time_own = lax.dynamic_slice_in_dim(timesteps[:, 0], z * own_masked, own_masked, 1)
    time_flat = time_own.reshape(row_count)
    embedded = frequency(time_flat).astype(bf16)
    time_pre, time_act, condition, cond_act = condition_forward(
        embedded, cond_in, time_in_weight, time_out_weight, cond_weight
    )
    abar_now, alpha_step, beta_step, beta_tilde, one_minus_now = plan(time_flat[:, None])
    start_own = lax.dynamic_slice_in_dim(targets[0], z * own_masked, own_masked, 0)
    start_rows = jnp.broadcast_to(start_own[None], (COPIES, own_masked, TOKCH)).reshape(
        row_count, TOKCH
    )
    eps_true = lax.dynamic_slice_in_dim(noise[:, 0], z * own_masked, own_masked, 1).reshape(
        row_count, TOKCH
    )
    noisy_rows = (jnp.sqrt(abar_now) * start_rows + jnp.sqrt(one_minus_now) * eps_true).astype(bf16)
    residual = product(noisy_rows, input_full)

    stored = []
    for l in range(DEPTH):
        scale, gate, pre, mod, block_out, following = layer_forward(
            residual, cond_act, *pack_of(l)
        )
        stored.append((residual, scale, gate, pre, mod, block_out))
        residual = following
    coef_diff = beta_step / jnp.sqrt(one_minus_now * alpha_step)
    coefs = jnp.concatenate(
        [jnp.log(beta_step), jnp.log(beta_tilde), coef_diff, jnp.zeros_like(coef_diff)], axis=1
    )

    grad_resid, grad_cact, final_grads, loss_tile, mean_part, var_part = final_layer(
        residual,
        cond_act,
        eps_true,
        coefs,
        out_full[:, :TOKCH],
        out_full[:, TOKCH:],
        second_pack,
        5 * (DEPTH - half_depth),
    )
    loss_total = loss_tile[0, 0]
    out_weight_part = jnp.concatenate([mean_part, var_part], axis=1)

    final_grad = jnp.moveaxis(reduce_pack(final_grads, z), 0, 1)
    where = jnp.stack([d, z]).astype(jnp.int32)
    reds = [None] * DEPTH
    grads = None
    for l in reversed(range(half_depth, DEPTH)):
        grad_resid, grad_cact, grads = layer_backward(
            where, grad_resid, stored[l], cond_act, grad_cact, *pack_of(l),
            grads, l - half_depth, DEPTH - half_depth,
        )
    summed = reduce_pack(grads, z)
    for l in range(half_depth, DEPTH):
        reds[l] = summed[5 * (l - half_depth) : 5 * (l - half_depth) + 5]
    for l in reversed(range(half_depth)):
        grad_resid, grad_cact, keep, send = layer_backward(
            where, grad_resid, stored[l], cond_act, grad_cact, *pack_of(l), None, 0, 0
        )
        reds[l] = reduce_halves(keep, send)
    ada_grad = jnp.stack([jnp.moveaxis(red[:3], 0, 1) for red in reds])
    in_grad = jnp.stack([red[3] for red in reds])
    out_grad = jnp.stack([red[4].T for red in reds])
    input_weight_part = product_tn(noisy_rows, grad_resid.astype(bf16))

    grad_cond_in, *thin = condition_backward(
        grad_cact, condition, time_pre, time_act, embedded, cond_in, time_out_weight, cond_weight
    )
    thin = jnp.concatenate([part.reshape(n, part.shape[0] // n, HW) for part in thin], axis=1)
    thin = relabel(thin, 0, n, d)
    thin_red = reduce_dp(thin[::2], thin[1::2])
    for bit in bit_list(t):
        thin_low = thin_red.astype(bf16)
        thin_red = thin_low.astype(f32) + flip(thin_low, "tensor", bit).astype(f32)
    marks = [HW // n, HW // n + FREQ // n]
    time_out_grad, time_in_grad, cond_grad = jnp.split(thin_red, marks, axis=0)

    grad_in_all = jnp.concatenate(gather_blocks(grad_cond_in), axis=0)
    grad_mlp = jnp.zeros((token_count, model_width), bf16).at[index_all].add(grad_in_all)
    grad_act_mlp = product_nt(grad_mlp, fc_out_weight)
    grad_mlp_pre = jax.vjp(partial(jax.nn.gelu, approximate=False), mlp_pre)[1](grad_act_mlp)[
        0
    ].astype(bf16)
    grad_normed_two = scatter_sum(row_blocks(product_nt(grad_mlp_pre, fc_in_weight)))
    ln2_gain_part = jnp.sum(grad_normed_two * normal_two, axis=0)
    ln2_bias_part = jnp.sum(grad_normed_two, axis=0)
    grad_middle = grad_mlp[:own_rows].astype(f32) + norm_back(
        grad_normed_two * ln2_gain, normal_two, inverse_two
    )
    grad_attn = jnp.concatenate(gather_blocks(grad_middle.astype(bf16)), axis=0)
    grad_attn_out = (
        product_nt(grad_attn, proj_weight).astype(bf16).reshape(token_count, head_count, HEAD)
    )
    value_grad = jnp.einsum("hqk,qhd->khd", prob_low, grad_attn_out, preferred_element_type=f32)
    grad_prob = jnp.einsum("qhd,khd->hqk", grad_attn_out, value_rows, preferred_element_type=f32)
    row_delta = jnp.sum(probability * grad_prob, axis=-1, keepdims=True)
    grad_scores = (probability * (grad_prob - row_delta)).astype(bf16)
    query_grad = (
        jnp.einsum("hqk,khd->qhd", grad_scores, key_rows, preferred_element_type=f32) * score_scale
    )
    key_grad = (
        jnp.einsum("hqk,qhd->khd", grad_scores, queries, preferred_element_type=f32) * score_scale
    )
    grad_qkv = jnp.concatenate(
        [
            query_grad.reshape(token_count, local_width),
            key_grad.reshape(token_count, local_width),
            value_grad.reshape(token_count, local_width),
        ],
        axis=1,
    ).astype(bf16)
    grad_normed_one = scatter_sum(row_blocks(product_nt(grad_qkv, qkv_flat)))
    own_normal = normal_one[:own_rows]
    ln1_gain_part = jnp.sum(grad_normed_one * own_normal, axis=0)
    ln1_bias_part = jnp.sum(grad_normed_one, axis=0)
    input_own = grad_middle + norm_back(
        grad_normed_one * ln1_gain, own_normal, inverse_one[:own_rows]
    )
    input_grad = relabel(
        jnp.concatenate(gather_blocks(input_own.astype(bf16)), axis=0), 0, t, z
    ).astype(f32)

    whole_grads = jnp.concatenate(
        [
            product_tn(attn_in, grad_qkv),
            product_tn(grad_attn, attn_out),
            product_tn(mlp_in, grad_mlp_pre),
            product_tn(grad_mlp, activated),
        ],
        axis=1,
    )
    whole_grads = relabel(
        whole_grads.astype(bf16).reshape(n, model_width // n, whole_grads.shape[1]), 0, n, d
    )
    block_red = reduce_dp(whole_grads[::2], whole_grads[1::2])
    marks = [3 * local_width, 4 * local_width, 4 * local_width + fc_in_weight.shape[1]]
    qkv_red, proj_red, fc_in_red, fc_out_red = jnp.split(block_red, marks, axis=1)

    lane_parts = jnp.concatenate(
        [
            ln1_gain_part,
            ln1_bias_part,
            ln2_gain_part,
            ln2_bias_part,
            jnp.full((128,), loss_total, f32),
        ]
    )
    input_weight_part = relabel(input_weight_part, 1, t, z)
    out_weight_part = relabel(out_weight_part, 0, t, z)
    shard_parts = [
        jnp.concatenate(
            [
                input_weight_part[:, r * hid : (r + 1) * hid].reshape(-1),
                out_weight_part[r * hid : (r + 1) * hid].reshape(-1),
            ]
        )
        for r in range(t)
    ]
    shard_own = shard_parts[0]
    for r in range(1, t):
        shard_own = shard_own + flip(shard_parts[r], "tensor", r)
    small = butterfly(jnp.concatenate([butterfly(lane_parts, "tensor"), shard_own]), "dp")
    lanes = 4 * model_width + 128
    edge = lanes + TOKCH * hid
    loss_mean = small[4 * model_width] / (n * t * row_count)
    return (
        loss_mean,
        hidden_out,
        input_grad,
        small[:model_width],
        small[model_width : 2 * model_width],
        qkv_red.reshape(model_width // n, 3, local_width),
        proj_red.T,
        small[2 * model_width : 3 * model_width],
        small[3 * model_width : 4 * model_width],
        fc_in_red,
        fc_out_red.T,
        cond_grad,
        time_in_grad,
        time_out_grad,
        small[lanes:edge].reshape(TOKCH, hid),
        ada_grad,
        in_grad,
        out_grad,
        final_grad,
        small[edge:].reshape(out_weight.shape),
    )


def solution(mesh):
    placed = (
        P("dp", None),
        P("dp", None),
        P("dp", None),
        P("dp", None),
        P("dp", None, None),
        P(None, "dp", None, None),
        P(None, "dp", None),
        P(),
        P(),
        P(None, None, "tensor"),
        P("tensor", None),
        P(),
        P(),
        P(None, "tensor"),
        P("tensor", None),
        P(),
        P(),
        P(),
        P(None, "tensor"),
        P(None, None, None, "tensor"),
        P(None, None, "tensor"),
        P(None, "tensor", None),
        P(None, None, "tensor"),
        P("tensor", None),
    )
    return jax.shard_map(
        shards,
        mesh=mesh,
        in_specs=placed,
        out_specs=(
            P(),
            P("dp", None),
            P("dp", None),
            P(),
            P(),
            P("dp", None, "tensor"),
            P("tensor", "dp"),
            P(),
            P(),
            P("dp", "tensor"),
            P("tensor", "dp"),
            P("dp", None),
            P("dp", None),
            P("dp", None),
            P(None, "tensor"),
            P(None, "dp", None, "tensor"),
            P(None, "dp", "tensor"),
            P(None, "tensor", "dp"),
            P("dp", None, "tensor"),
            P("tensor", None),
        ),
        check_vma=False,
    )
```

time: 3420 us -> 1290 us (0.38)
  waiting for transfers between devices: 2560 us -> 646 us
  matrix products: 328 us -> 37 us
  blocking collectives: 278 us -> 0 us
  Pallas kernels: 0 us -> 264 us
  starting transfers between devices: 3.42 us -> 93.9 us
    reduce_scatter x22 -> x2, waiting for transfers between devices: 1530 us -> 0.04 us  [reduce_pack(): part = lax.psum_scatter(grads, 'dp', scatter_dimension=0, tiled=True)[0]]
    ppermute x0 -> x79, waiting for transfers between devices: none -> 439 us  [flip(): return lax.ppermute(values, axis, [(i, i ^ mask) for i in range(size)])]
    all_gather x12 -> x2, waiting for transfers between devices: 640 us -> 207 us  [gather_pack(): full = lax.all_gather(chunk, ('dp', 'tensor'), axis=0, tiled=False)]
    psum x6 -> x0, waiting for transfers between devices: 394 us -> none  [the longest x1 190 us: shards(): cond_grad_act = lax.psum(cond_partial, 'tensor')]
    dot_general x84 -> x17, matrix products: 321 us -> 33 us  [the longest x4 10.4 us: product_nt(): lax.dot_general(left_op, right_op, (((1,), (1,)), ((), ())), preferred_el...]
    psum x15 -> x0, blocking collectives: 278 us -> none  [the longest x14 253 us: row_sums(): return lax.psum((first_sum, second_sum), 'tensor')]
    pallas_call x0 -> x15, Pallas kernels: none -> 264 us  [the longest x6 154 us: layer_backward(): pl.pallas_call(partial(backward_kernel, split=split), grid_spec=pltpu.Pre...]
    ppermute x0 -> x79, starting transfers between devices: none -> 93.7 us  [flip(): return lax.ppermute(values, axis, [(i, i ^ mask) for i in range(size)])]
  transfers between devices with their start and end apart: 41 -> 83, of which waited for: 39 -> 43; matrix products, arithmetic and copies ran while one was open for 7% -> 18% of each run, Pallas kernels for 0% -> 16%
where the time goes in v1:
time: 1290 us; the launch traced here: 1280 us
  waiting for transfers between devices  646 us (50%)
  Pallas kernels  264 us (20%)
  other arithmetic  117 us (9%)
  local copies, waits for them, and re-layouts  108 us (8%)
  starting transfers between devices  93.9 us (7%)
  matrix products  37 us (3%)
  between operations  18 us (1%)
    ppermute x79, waiting for transfers between devices, flip(): return lax.ppermute(values, axis, [(i, i ^ mask) for i in range(size)])  439 us
    all_gather x2, waiting for transfers between devices, gather_pack(): full = lax.all_gather(chunk, ('dp', 'tensor'), axis=0, tiled=False)  207 us
    pallas_call x6, Pallas kernels, layer_backward(): pl.pallas_call(partial(backward_kernel, split=split), grid_spec=pltpu.Pre...  154 us
    ppermute x79, starting transfers between devices, flip(): return lax.ppermute(values, axis, [(i, i ^ mask) for i in range(size)])  93.7 us
    pallas_call x6, Pallas kernels, layer_forward(): pl.pallas_call(forward_kernel, grid=(2 * t,), in_specs=[whole((rows, HW))...  81.4 us
    another operation x9, other arithmetic  54.7 us
    unnamed x277, local copies, waits for them, and re-layouts  42.2 us
  transfers between devices with their start and end apart: 83, of which 43 were waited for; matrix products, arithmetic and copies ran while one was open for 18% of the time, Pallas kernels for 16%

profile of v1, /device:TPU:0, one launch (start us, length us, event | category | flops | bytes accessed | tf_op | source)
XLA Modules:
  0.0 1283.7 jit_solution(10738138110185737767)
XLA Ops:
  68.1 36.0 %collective-permute-done.4 = bf16[128,768]{1,0:T(8,128)(2,1)S(1)} collective-permute-done((bf16[128,768]{1,0:T(8,128)(2,1)S(1)}, bf16[128,768]{1,0:T(8,128)(2,1)S(1)}, u32[]{:S(2)}, u32[]{:S(2)}) %collective-permute-start.4) | collective-permute-done | bytes 196640 | tf_op jit(solution)/shard_map/ppermute | solution.py:45
  117.4 14.9 %collective-permute-done.7 = bf16[128,768]{1,0:T(8,128)(2,1)S(1)} collective-permute-done((bf16[128,768]{1,0:T(8,128)(2,1)S(1)}, bf16[128,768]{1,0:T(8,128)(2,1)S(1)}, u32[]{:S(2)}, u32[]{:S(2)}) %collective-permute-start.7) | collective-permute-done | bytes 196640 | tf_op jit(solution)/shard_map/ppermute | solution.py:45
  150.1 31.8 %collective-permute-done.10 = bf16[128,768]{1,0:T(8,128)(2,1)S(1)} collective-permute-done((bf16[128,768]{1,0:T(8,128)(2,1)S(1)}, bf16[128,768]{1,0:T(8,128)(2,1)S(1)}, u32[]{:S(2)}, u32[]{:S(2)}) %collective-permute-start.10) | collective-permute-done | bytes 196640 | tf_op jit(solution)/shard_map/ppermute | solution.py:45
  193.8 17.5 %collective-permute-done.13 = bf16[128,768]{1,0:T(8,128)(2,1)S(1)} collective-permute-done((bf16[128,768]{1,0:T(8,128)(2,1)S(1)}, bf16[128,768]{1,0:T(8,128)(2,1)S(1)}, u32[]{:S(2)}, u32[]{:S(2)}) %collective-permute-start.13) | collective-permute-done | bytes 196640 | tf_op jit(solution)/shard_map/ppermute | solution.py:45
  218.1 39.4 %all-gather.5.cloned.1.call-done = bf16[480,128,256]{2,1,0:T(8,128)(2,1)} async-done(((bf16[15,128,256]{2,1,0:T(8,128)(2,1)}), bf16[480,128,256]{2,1,0:T(8,128)(2,1)}) %all-gather.5.cloned.1.call-update) | async-done | bytes 31457296 | tf_op jit(solution)/shard_map/all_gather | solution.py:128
  257.5 13.5 %shard_map.384 = (f32[320,1024]{1,0:T(8,128)}, f32[320,1024]{1,0:T(8,128)}, f32[320,1024]{1,0:T(8,128)}, bf16[320,1024]{1,0:T(8,128)(2,1)}, f32[320,1024]{1,0:T(8,128)}, /*index=5*/f32[320,1024]{1,0:T(8,128)}) custom-call(f32[320,1024]{1,0:T(8,128)} %fusion.112.resid_ref, bf16[320,1024]{1,0:T(8,128)(2,1)} %get-tuple-element.91.cond_ref, ...), custom_call_target="tpu_custom_call" | custom-call | flops 3355443200 | bytes 20316160 | tf_op jit(solution)/shard_map/pallas_call | solution.py:242
  271.0 13.5 %shard_map.385 = (f32[320,1024]{1,0:T(8,128)}, f32[320,1024]{1,0:T(8,128)}, f32[320,1024]{1,0:T(8,128)}, bf16[320,1024]{1,0:T(8,128)(2,1)}, f32[320,1024]{1,0:T(8,128)}, /*index=5*/f32[320,1024]{1,0:T(8,128)}) custom-call(f32[320,1024]{1,0:T(8,128)} %get-tuple-element.92.resid_ref, bf16[320,1024]{1,0:T(8,128)(2,1)} %get-tuple-element.91.cond_ref, ...), custom_call_target="tpu_custom_call" | custom-call | flops 3355443200 | bytes 20316160 | tf_op jit(solution)/shard_map/pallas_call | solution.py:242
  284.5 13.5 %shard_map.386 = (f32[320,1024]{1,0:T(8,128)}, f32[320,1024]{1,0:T(8,128)}, f32[320,1024]{1,0:T(8,128)}, bf16[320,1024]{1,0:T(8,128)(2,1)}, f32[320,1024]{1,0:T(8,128)}, /*index=5*/f32[320,1024]{1,0:T(8,128)}) custom-call(f32[320,1024]{1,0:T(8,128)} %get-tuple-element.93.resid_ref, bf16[320,1024]{1,0:T(8,128)(2,1)} %get-tuple-element.91.cond_ref, ...), custom_call_target="tpu_custom_call" | custom-call | flops 3355443200 | bytes 20316160 | tf_op jit(solution)/shard_map/pallas_call | solution.py:242
  298.0 167.2 %all-gather.7.cloned.1.call-done = bf16[544,128,256]{2,1,0:T(8,128)(2,1)} async-done(((bf16[17,128,256]{2,1,0:T(8,128)(2,1)}), bf16[544,128,256]{2,1,0:T(8,128)(2,1)}) %all-gather.7.cloned.1.call-update) | async-done | bytes 35651600 | tf_op jit(solution)/shard_map/all_gather | solution.py:128
  465.2 14.0 %shard_map.387 = (f32[320,1024]{1,0:T(8,128)}, f32[320,1024]{1,0:T(8,128)}, f32[320,1024]{1,0:T(8,128)}, bf16[320,1024]{1,0:T(8,128)(2,1)}, f32[320,1024]{1,0:T(8,128)}, /*index=5*/f32[320,1024]{1,0:T(8,128)}) custom-call(f32[320,1024]{1,0:T(8,128)} %get-tuple-element.94.resid_ref, bf16[320,1024]{1,0:T(8,128)(2,1)} %get-tuple-element.91.cond_ref, ...), custom_call_target="tpu_custom_call" | custom-call | flops 3355443200 | bytes 20316160 | tf_op jit(solution)/shard_map/pallas_call | solution.py:242
  479.2 13.4 %shard_map.388 = (f32[320,1024]{1,0:T(8,128)}, f32[320,1024]{1,0:T(8,128)}, f32[320,1024]{1,0:T(8,128)}, bf16[320,1024]{1,0:T(8,128)(2,1)}, f32[320,1024]{1,0:T(8,128)}, /*index=5*/f32[320,1024]{1,0:T(8,128)}) custom-call(f32[320,1024]{1,0:T(8,128)} %get-tuple-element.95.resid_ref, bf16[320,1024]{1,0:T(8,128)(2,1)} %get-tuple-element.91.cond_ref, ...), custom_call_target="tpu_custom_call" | custom-call | flops 3355443200 | bytes 20316160 | tf_op jit(solution)/shard_map/pallas_call | solution.py:242
  492.6 13.5 %shard_map.389 = (f32[320,1024]{1,0:T(8,128)}, f32[320,1024]{1,0:T(8,128)}, f32[320,1024]{1,0:T(8,128)}, bf16[320,1024]{1,0:T(8,128)(2,1)}, f32[320,1024]{1,0:T(8,128)}, /*index=5*/f32[320,1024]{1,0:T(8,128)}) custom-call(f32[320,1024]{1,0:T(8,128)} %get-tuple-element.96.resid_ref, bf16[320,1024]{1,0:T(8,128)(2,1)} %get-tuple-element.91.cond_ref, ...), custom_call_target="tpu_custom_call" | custom-call | flops 3355443200 | bytes 20316160 | tf_op jit(solution)/shard_map/pallas_call | solution.py:242
  506.2 14.5 %shard_map.390 = (f32[320,1024]{1,0:T(8,128)}, f32[320,1024]{1,0:T(8,128)}, bf16[8,4,2,128,256]{4,3,2,1,0:T(8,128)(2,1)}, f32[8,128]{1,0:T(8,128)}, f32[1024,16]{1,0:T(8,128)}, /*index=5*/f32[1024,16]{1,0:T(8,128)}) custom-call(f32[320,1024]{1,0:T(8,128)} %get-tuple-element.97.resid_ref, bf16[320,1024]{1,0:T(8,128)(2,1)} %get-tuple-element.91.cond_ref, ...), custom_call_target="tpu_custom_call" | custom-call | flops 4026531840 | bytes 14942208 | tf_op jit(solution)/shard_map/pallas_call | solution.py:456
  521.4 23.1 %shard_map.391 = (f32[320,1024]{1,0:T(8,128)}, f32[320,1024]{1,0:T(8,128)}, bf16[8,4,15,128,256]{4,3,2,1,0:T(8,128)(2,1)}) custom-call(s32[2]{0:T(128)} %pad_add_fusion.1.where_ref, f32[320,1024]{1,0:T(8,128)} %get-tuple-element.98.gres_ref, f32[320,1024]{1,0:T(8,128)} %get-tuple-element.96.resid_ref, f32[320,1024]{1,0:T(8,128)} %get-tuple-element.99.scale_ref, ...), custom_call_target="tpu_custom_call" | custom-call | flops 6710886400 | bytes 34078720 | tf_op jit(solution)/shard_map/pallas_call | solution.py:359
  544.4 22.3 %shard_map.392 = (f32[320,1024]{1,0:T(8,128)}, f32[320,1024]{1,0:T(8,128)}, bf16[8,4,15,128,256]{4,3,2,1,0:T(8,128)(2,1)}) custom-call(s32[2]{0:T(128)} %pad_add_fusion.1.where_ref, f32[320,1024]{1,0:T(8,128)} %get-tuple-element.105.gres_ref, f32[320,1024]{1,0:T(8,128)} %get-tuple-element.95.resid_ref, ...), custom_call_target="tpu_custom_call", output_to_operand_aliasing={{2}: (15, {})} | custom-call | flops 6710886400 | bytes 34078720 | tf_op jit(solution)/shard_map/pallas_call | solution.py:359
  566.8 22.5 %shard_map.393 = (f32[320,1024]{1,0:T(8,128)}, f32[320,1024]{1,0:T(8,128)}, bf16[8,4,15,128,256]{4,3,2,1,0:T(8,128)(2,1)}) custom-call(s32[2]{0:T(128)} %pad_add_fusion.1.where_ref, f32[320,1024]{1,0:T(8,128)} %get-tuple-element.113.gres_ref, f32[320,1024]{1,0:T(8,128)} %get-tuple-element.94.resid_ref, ...), custom_call_target="tpu_custom_call", output_to_operand_aliasing={{2}: (15, {})} | custom-call | flops 6710886400 | bytes 34078720 | tf_op jit(solution)/shard_map/pallas_call | solution.py:359
  592.1 29.8 %shard_map.394 = (f32[320,1024]{1,0:T(8,128)}, f32[320,1024]{1,0:T(8,128)}, bf16[4,4,5,128,256]{4,3,2,1,0:T(8,128)(2,1)}, bf16[4,4,5,128,256]{4,3,2,1,0:T(8,128)(2,1)}) custom-call(s32[2]{0:T(128)} %pad_add_fusion.1.where_ref, f32[320,1024]{1,0:T(8,128)} %get-tuple-element.121.gres_ref, f32[320,1024]{1,0:T(8,128)} %get-tuple-element.93.resid_ref, ...), custom_call_target="tpu_custom_call" | custom-call | flops 6710886400 | bytes 34078720 | tf_op jit(solution)/shard_map/pallas_call | solution.py:359
  621.9 28.8 %shard_map.395 = (f32[320,1024]{1,0:T(8,128)}, f32[320,1024]{1,0:T(8,128)}, bf16[4,4,5,128,256]{4,3,2,1,0:T(8,128)(2,1)}, bf16[4,4,5,128,256]{4,3,2,1,0:T(8,128)(2,1)}) custom-call(s32[2]{0:T(128)} %pad_add_fusion.1.where_ref, f32[320,1024]{1,0:T(8,128)} %get-tuple-element.128.gres_ref, f32[320,1024]{1,0:T(8,128)} %get-tuple-element.92.resid_ref, ...), custom_call_target="tpu_custom_call" | custom-call | flops 6710886400 | bytes 34078720 | tf_op jit(solution)/shard_map/pallas_call | solution.py:359
  650.7 27.6 %shard_map.396 = (f32[320,1024]{1,0:T(8,128)}, f32[320,1024]{1,0:T(8,128)}, bf16[4,4,5,128,256]{4,3,2,1,0:T(8,128)(2,1)}, bf16[4,4,5,128,256]{4,3,2,1,0:T(8,128)(2,1)}) custom-call(s32[2]{0:T(128)} %pad_add_fusion.1.where_ref, f32[320,1024]{1,0:T(8,128)} %get-tuple-element.135.gres_ref, f32[320,1024]{1,0:T(8,128)} %fusion.112.resid_ref, ...), custom_call_target="tpu_custom_call" | custom-call | flops 6710886400 | bytes 34078720 | tf_op jit(solution)/shard_map/pallas_call | solution.py:359
  837.4 32.1 %collective-permute-done.36 = f32[15488]{0:T(1024)S(1)} collective-permute-done((f32[15488]{0:T(1024)S(1)}, f32[15488]{0:T(1024)S(1)}, u32[]{:S(2)}, u32[]{:S(2)}) %collective-permute-start.36) | collective-permute-done | bytes 61984 | tf_op jit(solution)/shard_map/ppermute | solution.py:45
  890.3 12.2 collective-permute-done.46
  928.6 17.6 %collective-permute-done.48 = bf16[256,1024]{1,0:T(8,128)(2,1)} collective-permute-done((bf16[256,1024]{1,0:T(8,128)(2,1)}, bf16[256,1024]{1,0:T(8,128)(2,1)}, u32[]{:S(2)}, u32[]{:S(2)}) %collective-permute-start.48) | collective-permute-done | bytes 524320 | tf_op jit(solution)/shard_map/ppermute | solution.py:45
  949.9 12.3 fusion.155
  969.2 12.3 fusion.156
  986.2 12.3 fusion.157
  1031.0 22.9 %collective-permute-done.69 = bf16[2,2,5,128,256]{4,3,2,1,0:T(8,128)(2,1)} collective-permute-done((bf16[2,2,5,128,256]{4,3,2,1,0:T(8,128)(2,1)}, bf16[2,2,5,128,256]{4,3,2,1,0:T(8,128)(2,1)}, u32[]{:S(2)}, u32[]{:S(2)}) %collective-permute-start.69) | collective-permute-done | bytes 1310752 | tf_op jit(solution)/shard_map/ppermute | solution.py:45
  1072.4 33.3 %collective-permute-done.62 = bf16[1,2,5,128,256]{4,3,2,1,0:T(8,128)(2,1)S(1)} collective-permute-done((bf16[1,2,5,128,256]{4,3,2,1,0:T(8,128)(2,1)S(1)}, bf16[1,2,5,128,256]{4,3,2,1,0:T(8,128)(2,1)S(1)}, u32[]{:S(2)}, u32[]{:S(2)}) %collective-permute-start.62) | collective-permute-done | bytes 655392 | tf_op jit(solution)/shard_map/ppermute | solution.py:45
  1122.4 11.6 collective-permute-done.59
  1150.5 10.1 collective-permute-done.52
  1163.5 11.6 collective-permute-done.60
  1185.8 35.4 %collective-permute-done.73 = bf16[15,128,256]{2,1,0:T(8,128)(2,1)S(1)} collective-permute-done((bf16[15,128,256]{2,1,0:T(8,128)(2,1)S(1)}, bf16[15,128,256]{2,1,0:T(8,128)(2,1)S(1)}, u32[]{:S(2)}, u32[]{:S(2)}) %collective-permute-start.73) | collective-permute-done | bytes 983072 | tf_op jit(solution)/shard_map/ppermute | solution.py:45
  1226.9 38.5 %collective-permute-done.74 = bf16[15,128,256]{2,1,0:T(8,128)(2,1)S(1)} collective-permute-done((bf16[15,128,256]{2,1,0:T(8,128)(2,1)S(1)}, bf16[15,128,256]{2,1,0:T(8,128)(2,1)S(1)}, u32[]{:S(2)}, u32[]{:S(2)}) %collective-permute-start.74) | collective-permute-done | bytes 983072 | tf_op jit(solution)/shard_map/ppermute | solution.py:45
  (631 shorter events, 446.6 us)
Async XLA Ops:
  7.2 250.3 %all-gather.5.cloned.1.call-start = ((), (), s32[]{:S(2)}) async-start(), calls=%async_computation.4 | async-start | bytes 32440320 | tf_op jit(solution)/shard_map/all_gather | solution.py:128
  18.8 446.4 %all-gather.7.cloned.1.call-start = ((), (), s32[]{:S(2)}) async-start(), calls=%async_computation.5 | async-start | bytes 36765696 | tf_op jit(solution)/shard_map/all_gather | solution.py:128
  21.1 983.7 %reduce-scatter.5.cloned.1.call-start = ((), (), s32[]{:S(2)}) async-start(), calls=%async_computation.3 | async-start | bytes 4718592 | tf_op jit(solution)/shard_map/reduce_scatter | solution.py:133
  21.2 35.5 %collective-permute-start.1 = (bf16[16,256]{1,0:T(8,128)(2,1)}, bf16[16,256]{1,0:T(8,128)(2,1)}, u32[]{:S(2)}, u32[]{:S(2)}) collective-permute-start(bf16[16,256]{1,0:T(8,128)(2,1)} %param.42), channel_id=1, source_target_pairs={{0,2},{1,3},{2,0},{3,1},{4,6},{5,7},{6,4},{7,5},{8,10},{9,11},{10,... | collective-permute-start | bytes 24584 | tf_op jit(solution)/shard_map/ppermute | solution.py:45
  26.8 83.3 %collective-permute-start.16 = (bf16[256,32]{0,1:T(8,128)(2,1)}, bf16[256,32]{0,1:T(8,128)(2,1)}, u32[]{:S(2)}, u32[]{:S(2)}) collective-permute-start(bf16[256,32]{0,1:T(8,128)(2,1)} %param.47), channel_id=1, source_target_pairs={{0,2},{1,3},{2,0},{3,1},{4,6},{5,7},{6,4},{7,5},{8,10},{9,11},{10,... | collective-permute-start | bytes 49160 | tf_op jit(solution)/shard_map/ppermute | solution.py:45
  28.7 36.1 %collective-permute-start.15 = (bf16[256,32]{0,1:T(8,128)(2,1)}, bf16[256,32]{0,1:T(8,128)(2,1)}, u32[]{:S(2)}, u32[]{:S(2)}) collective-permute-start(bf16[256,32]{0,1:T(8,128)(2,1)} %param.47), channel_id=1, source_target_pairs={{0,1},{1,0},{2,3},{3,2},{4,5},{5,4},{6,7},{7,6},{8,9},{9,8},{10,11... | collective-permute-start | bytes 49160 | tf_op jit(solution)/shard_map/ppermute | solution.py:45
  59.4 44.7 %collective-permute-start.4 = (bf16[128,768]{1,0:T(8,128)(2,1)S(1)}, bf16[128,768]{1,0:T(8,128)(2,1)S(1)}, u32[]{:S(2)}, u32[]{:S(2)}) collective-permute-start(bf16[128,768]{1,0:T(8,128)(2,1)S(1)} %get-tuple-element.312), channel_id=1, source_target_pairs={{0,2},{1,3},{2,0},{3,1},{4,6},{5,7},{6,4},{7,5},{8,10},{9,11},{10,... | collective-permute-start | bytes 589832 | tf_op jit(solution)/shard_map/ppermute | solution.py:45
  64.8 46.1 %collective-permute-start.17 = (bf16[256,32]{0,1:T(8,128)(2,1)}, bf16[256,32]{0,1:T(8,128)(2,1)S(1)}, u32[]{:S(2)}, u32[]{:S(2)}) collective-permute-start(bf16[256,32]{0,1:T(8,128)(2,1)} %param.47), channel_id=1, source_target_pairs={{0,3},{1,2},{2,1},{3,0},{4,7},{5,6},{6,5},{7,4},{8,11},{9,10},{10,... | collective-permute-start | bytes 49160 | tf_op jit(solution)/shard_map/ppermute | solution.py:45
  141.4 40.5 %collective-permute-start.10 = (bf16[128,768]{1,0:T(8,128)(2,1)S(1)}, bf16[128,768]{1,0:T(8,128)(2,1)S(1)}, u32[]{:S(2)}, u32[]{:S(2)}) collective-permute-start(bf16[128,768]{1,0:T(8,128)(2,1)S(1)} %get-tuple-element.309), channel_id=1, source_target_pairs={{0,2},{1,3},{2,0},{3,1},{4,6},{5,7},{6,4},{7,5},{8,10},{9,11},{10,... | collective-permute-start | bytes 589832 | tf_op jit(solution)/shard_map/ppermute | solution.py:45
  520.7 658.1 %reduce-scatter.3.cloned.1.call-start = ((), (), s32[]{:S(2)}) async-start(), calls=%async_computation.2 | async-start | bytes 35389440 | tf_op jit(solution)/shard_map/reduce_scatter | solution.py:133
  708.9 107.9 %collective-permute-start.44 = (bf16[4,256,1024]{2,1,0:T(8,128)(2,1)}, bf16[4,256,1024]{2,1,0:T(8,128)(2,1)}, u32[]{:S(2)}, u32[]{:S(2)}) collective-permute-start(bf16[4,256,1024]{2,1,0:T(8,128)(2,1)} %slice.529), channel_id=1, source_target_pairs={{0,4},{4,0},{8,12},{12,8},{16,20},{20,16},{24,28},{28,24},{1,5},{5... | collective-permute-start | bytes 6291464 | tf_op jit(solution)/shard_map/ppermute | solution.py:45
  709.0 240.9 %collective-permute-start.49 = (bf16[4,4,5,128,256]{4,3,2,1,0:T(8,128)(2,1)}, bf16[4,4,5,128,256]{4,3,2,1,0:T(8,128)(2,1)}, u32[]{:S(2)}, u32[]{:S(2)}) collective-permute-start(bf16[4,4,5,128,256]{4,3,2,1,0:T(8,128)(2,1)} %get-tuple-element.155), channel_id=1, source_target_pairs={{0,4},{4,0},{8,12},{12,8},{16,20},{20,16},{24,28},{28,24},{1,5},{5... | collective-permute-start | bytes 15728648 | tf_op jit(solution)/shard_map/ppermute | solution.py:45
  811.4 58.0 %collective-permute-start.40 = (bf16[128,768]{1,0:T(8,128)(2,1)}, bf16[128,768]{1,0:T(8,128)(2,1)}, u32[]{:S(2)}, u32[]{:S(2)}) collective-permute-start(bf16[128,768]{1,0:T(8,128)(2,1)} %add_convert_fusion.3), channel_id=1, source_target_pairs={{0,3},{1,2},{2,1},{3,0},{4,7},{5,6},{6,5},{7,4},{8,11},{9,10},{10,... | collective-permute-start | bytes 589832 | tf_op jit(solution)/shard_map/ppermute | solution.py:45
  823.3 60.2 %collective-permute-start.45 = (bf16[2,256,1024]{2,1,0:T(8,128)(2,1)}, bf16[2,256,1024]{2,1,0:T(8,128)(2,1)}, u32[]{:S(2)}, u32[]{:S(2)}) collective-permute-start(bf16[2,256,1024]{2,1,0:T(8,128)(2,1)} %pad_maximum_fusion.6), channel_id=1, source_target_pairs={{0,8},{4,12},{8,0},{12,4},{16,24},{20,28},{24,16},{28,20},{1,9},{5... | collective-permute-start | bytes 3145736 | tf_op jit(solution)/shard_map/ppermute | solution.py:45
  834.4 53.1 %collective-permute-start.42 = (bf16[2,96,2304]{2,1,0:T(8,128)(2,1)}, bf16[2,96,2304]{2,1,0:T(8,128)(2,1)S(1)}, u32[]{:S(2)}, u32[]{:S(2)}) collective-permute-start(bf16[2,96,2304]{2,1,0:T(8,128)(2,1)} %copy.128), channel_id=1, source_target_pairs={{0,8},{4,12},{8,0},{12,4},{16,24},{20,28},{24,16},{28,20},{1,9},{5... | collective-permute-start | bytes 2654216 | tf_op jit(solution)/shard_map/ppermute | solution.py:45
  880.7 88.5 %collective-permute-start.57 = (bf16[4,4,5,128,256]{4,3,2,1,0:T(8,128)(2,1)}, bf16[4,4,5,128,256]{4,3,2,1,0:T(8,128)(2,1)}, u32[]{:S(2)}, u32[]{:S(2)}) collective-permute-start(bf16[4,4,5,128,256]{4,3,2,1,0:T(8,128)(2,1)} %get-tuple-element.157), channel_id=1, source_target_pairs={{0,4},{4,0},{8,12},{12,8},{16,20},{20,16},{24,28},{28,24},{1,5},{5... | collective-permute-start | bytes 15728648 | tf_op jit(solution)/shard_map/ppermute | solution.py:45
  881.0 105.1 %collective-permute-start.65 = (bf16[4,4,5,128,256]{4,3,2,1,0:T(8,128)(2,1)}, bf16[4,4,5,128,256]{4,3,2,1,0:T(8,128)(2,1)}, u32[]{:S(2)}, u32[]{:S(2)}) collective-permute-start(bf16[4,4,5,128,256]{4,3,2,1,0:T(8,128)(2,1)} %get-tuple-element.159), channel_id=1, source_target_pairs={{0,4},{4,0},{8,12},{12,8},{16,20},{20,16},{24,28},{28,24},{1,5},{5... | collective-permute-start | bytes 15728648 | tf_op jit(solution)/shard_map/ppermute | solution.py:45
  967.3 89.7 %collective-permute-start.50 = (bf16[2,2,5,128,256]{4,3,2,1,0:T(8,128)(2,1)}, bf16[2,2,5,128,256]{4,3,2,1,0:T(8,128)(2,1)}, u32[]{:S(2)}, u32[]{:S(2)}) collective-permute-start(bf16[2,2,5,128,256]{4,3,2,1,0:T(8,128)(2,1)} %pad_maximum_fusion.2), channel_id=1, source_target_pairs={{0,8},{4,12},{8,0},{12,4},{16,24},{20,28},{24,16},{28,20},{1,9},{5... | collective-permute-start | bytes 3932168 | tf_op jit(solution)/shard_map/ppermute | solution.py:45
  967.9 45.0 %collective-permute-start.53 = (bf16[2,2,5,128,256]{4,3,2,1,0:T(8,128)(2,1)}, bf16[2,2,5,128,256]{4,3,2,1,0:T(8,128)(2,1)}, u32[]{:S(2)}, u32[]{:S(2)}) collective-permute-start(bf16[2,2,5,128,256]{4,3,2,1,0:T(8,128)(2,1)} %slice.661), channel_id=1, source_target_pairs={{0,16},{4,20},{8,24},{12,28},{16,0},{20,4},{24,8},{28,12},{1,17},{... | collective-permute-start | bytes 3932168 | tf_op jit(solution)/shard_map/ppermute | solution.py:45
  984.1 43.9 %collective-permute-start.61 = (bf16[2,2,5,128,256]{4,3,2,1,0:T(8,128)(2,1)}, bf16[2,2,5,128,256]{4,3,2,1,0:T(8,128)(2,1)}, u32[]{:S(2)}, u32[]{:S(2)}) collective-permute-start(bf16[2,2,5,128,256]{4,3,2,1,0:T(8,128)(2,1)} %slice.677), channel_id=1, source_target_pairs={{0,16},{4,20},{8,24},{12,28},{16,0},{20,4},{24,8},{28,12},{1,17},{... | collective-permute-start | bytes 3932168 | tf_op jit(solution)/shard_map/ppermute | solution.py:45
  1000.9 53.0 %collective-permute-start.69 = (bf16[2,2,5,128,256]{4,3,2,1,0:T(8,128)(2,1)}, bf16[2,2,5,128,256]{4,3,2,1,0:T(8,128)(2,1)}, u32[]{:S(2)}, u32[]{:S(2)}) collective-permute-start(bf16[2,2,5,128,256]{4,3,2,1,0:T(8,128)(2,1)} %slice.693), channel_id=1, source_target_pairs={{0,16},{4,20},{8,24},{12,28},{16,0},{20,4},{24,8},{28,12},{1,17},{... | collective-permute-start | bytes 3932168 | tf_op jit(solution)/shard_map/ppermute | solution.py:45
  1017.8 52.7 %collective-permute-start.58 = (bf16[2,2,5,128,256]{4,3,2,1,0:T(8,128)(2,1)S(1)}, bf16[2,2,5,128,256]{4,3,2,1,0:T(8,128)(2,1)S(1)}, u32[]{:S(2)}, u32[]{:S(2)}) collective-permute-start(bf16[2,2,5,128,256]{4,3,2,1,0:T(8,128)(2,1)S(1)} %copy-done.27), channel_id=1, source_target_pairs={{0,8},{4,12},{8,0},{12,4},{16,24},{20,28},{24,16},{28,20},{1,9},{5... | collective-permute-start | bytes 3932168 | tf_op jit(solution)/shard_map/ppermute | solution.py:45
  1022.4 41.1 %collective-permute-start.54 = (bf16[1,2,5,128,256]{4,3,2,1,0:T(8,128)(2,1)S(1)}, bf16[1,2,5,128,256]{4,3,2,1,0:T(8,128)(2,1)S(1)}, u32[]{:S(2)}, u32[]{:S(2)}) collective-permute-start(bf16[1,2,5,128,256]{4,3,2,1,0:T(8,128)(2,1)S(1)} %fusion.23), channel_id=1, source_target_pairs={{0,8},{4,12},{8,0},{12,4},{16,24},{20,28},{24,16},{28,20},{1,9},{5... | collective-permute-start | bytes 1966088 | tf_op jit(solution)/shard_map/ppermute | solution.py:45
  1028.0 80.8 %collective-permute-start.66 = (bf16[2,2,5,128,256]{4,3,2,1,0:T(8,128)(2,1)S(1)}, bf16[2,2,5,128,256]{4,3,2,1,0:T(8,128)(2,1)S(1)}, u32[]{:S(2)}, u32[]{:S(2)}) collective-permute-start(bf16[2,2,5,128,256]{4,3,2,1,0:T(8,128)(2,1)S(1)} %pad_maximum_fusion.4), channel_id=1, source_target_pairs={{0,8},{4,12},{8,0},{12,4},{16,24},{20,28},{24,16},{28,20},{1,9},{5... | collective-permute-start | bytes 3932168 | tf_op jit(solution)/shard_map/ppermute | solution.py:45
  1053.9 51.8 %collective-permute-start.62 = (bf16[1,2,5,128,256]{4,3,2,1,0:T(8,128)(2,1)S(1)}, bf16[1,2,5,128,256]{4,3,2,1,0:T(8,128)(2,1)S(1)}, u32[]{:S(2)}, u32[]{:S(2)}) collective-permute-start(bf16[1,2,5,128,256]{4,3,2,1,0:T(8,128)(2,1)S(1)} %fusion.18), channel_id=1, source_target_pairs={{0,8},{4,12},{8,0},{12,4},{16,24},{20,28},{24,16},{28,20},{1,9},{5... | collective-permute-start | bytes 1966088 | tf_op jit(solution)/shard_map/ppermute | solution.py:45
  1057.0 57.8 %collective-permute-start.70 = (bf16[1,2,5,128,256]{4,3,2,1,0:T(8,128)(2,1)S(1)}, bf16[1,2,5,128,256]{4,3,2,1,0:T(8,128)(2,1)S(1)}, u32[]{:S(2)}, u32[]{:S(2)}) collective-permute-start(bf16[1,2,5,128,256]{4,3,2,1,0:T(8,128)(2,1)S(1)} %fusion.13), channel_id=1, source_target_pairs={{0,8},{4,12},{8,0},{12,4},{16,24},{20,28},{24,16},{28,20},{1,9},{5... | collective-permute-start | bytes 1966088 | tf_op jit(solution)/shard_map/ppermute | solution.py:45
  1066.2 79.8 %collective-permute-start.55 = (bf16[5,128,256]{2,1,0:T(8,128)(2,1)S(1)}, bf16[5,128,256]{2,1,0:T(8,128)(2,1)S(1)}, u32[]{:S(2)}, u32[]{:S(2)}) collective-permute-start(bf16[5,128,256]{2,1,0:T(8,128)(2,1)S(1)} %get-tuple-element.321), channel_id=1, source_target_pairs={{0,2},{1,3},{2,0},{3,1},{4,6},{5,7},{6,4},{7,5},{8,10},{9,11},{10,... | collective-permute-start | bytes 983048 | tf_op jit(solution)/shard_map/ppermute | solution.py:45
  1070.5 78.1 %collective-permute-start.56 = (bf16[5,128,256]{2,1,0:T(8,128)(2,1)S(1)}, bf16[5,128,256]{2,1,0:T(8,128)(2,1)S(1)}, u32[]{:S(2)}, u32[]{:S(2)}) collective-permute-start(bf16[5,128,256]{2,1,0:T(8,128)(2,1)S(1)} %get-tuple-element.322), channel_id=1, source_target_pairs={{0,3},{1,2},{2,1},{3,0},{4,7},{5,6},{6,5},{7,4},{8,11},{9,10},{10,... | collective-permute-start | bytes 983048 | tf_op jit(solution)/shard_map/ppermute | solution.py:45
  1108.9 52.6 %collective-permute-start.63 = (bf16[5,128,256]{2,1,0:T(8,128)(2,1)S(1)}, bf16[5,128,256]{2,1,0:T(8,128)(2,1)S(1)}, u32[]{:S(2)}, u32[]{:S(2)}) collective-permute-start(bf16[5,128,256]{2,1,0:T(8,128)(2,1)S(1)} %get-tuple-element.319), channel_id=1, source_target_pairs={{0,2},{1,3},{2,0},{3,1},{4,6},{5,7},{6,4},{7,5},{8,10},{9,11},{10,... | collective-permute-start | bytes 983048 | tf_op jit(solution)/shard_map/ppermute | solution.py:45
  1180.8 40.4 %collective-permute-start.73 = (bf16[15,128,256]{2,1,0:T(8,128)(2,1)S(1)}, bf16[15,128,256]{2,1,0:T(8,128)(2,1)S(1)}, u32[]{:S(2)}, u32[]{:S(2)}) collective-permute-start(bf16[15,128,256]{2,1,0:T(8,128)(2,1)S(1)} %get-tuple-element.270), channel_id=1, source_target_pairs={{0,1},{1,0},{2,3},{3,2},{4,5},{5,4},{6,7},{7,6},{8,9},{9,8},{10,11... | collective-permute-start | bytes 2949128 | tf_op jit(solution)/shard_map/ppermute | solution.py:45
  1181.3 45.7 %collective-permute-start.75 = (bf16[15,128,256]{2,1,0:T(8,128)(2,1)S(1)}, bf16[15,128,256]{2,1,0:T(8,128)(2,1)S(1)}, u32[]{:S(2)}, u32[]{:S(2)}) collective-permute-start(bf16[15,128,256]{2,1,0:T(8,128)(2,1)S(1)} %get-tuple-element.271), channel_id=1, source_target_pairs={{0,3},{1,2},{2,1},{3,0},{4,7},{5,6},{6,5},{7,4},{8,11},{9,10},{10,... | collective-permute-start | bytes 2949128 | tf_op jit(solution)/shard_map/ppermute | solution.py:45
  1183.1 82.4 %collective-permute-start.74 = (bf16[15,128,256]{2,1,0:T(8,128)(2,1)S(1)}, bf16[15,128,256]{2,1,0:T(8,128)(2,1)S(1)}, u32[]{:S(2)}, u32[]{:S(2)}) collective-permute-start(bf16[15,128,256]{2,1,0:T(8,128)(2,1)S(1)} %get-tuple-element.272), channel_id=1, source_target_pairs={{0,2},{1,3},{2,0},{3,1},{4,6},{5,7},{6,4},{7,5},{8,10},{9,11},{10,... | collective-permute-start | bytes 2949128 | tf_op jit(solution)/shard_map/ppermute | solution.py:45
  (155 other events, 1931.0 us)
Sparse Core Ops, SparseCore 0:
  18.9 238.5 all-gather.4
  260.4 204.8 all-gather.6
  520.9 49.4 reduce-scatter.4
  589.5 187.6 reduce-scatter.2

commit v2 on v1

--- a/solution.py
+++ b/solution.py
@@ -15,6 +15,7 @@
 FREQ = 256
 COPIES = 4
 STEPS = 1000
+GROUPS = ((5, 4, 3), (2, 1, 0))
 
 norm_eps = 1e-06
 bf16 = jnp.bfloat16
@@ -129,14 +130,21 @@
     return full.reshape((lax.axis_size("dp"), lax.axis_size("tensor")) + chunk.shape)
 
 
-def reduce_pack(grads, z):
-    part = lax.psum_scatter(grads, "dp", scatter_dimension=0, tiled=True)[0]
+def reduce_over_dp(grads):
+    return lax.psum_scatter(grads, "dp", scatter_dimension=0, tiled=True)[0]
+
+
+def reduce_tensor(part, z):
     return scatter_sum(
         [
             lax.dynamic_index_in_dim(part, z ^ r, axis=0, keepdims=False)
-            for r in range(grads.shape[1])
+            for r in range(part.shape[0])
         ]
     )
+
+
+def after(value, *arrived):
+    return lax.optimization_barrier((value,) + arrived)[0]
 
 
 def reduce_outer(alive, order):
@@ -153,16 +161,6 @@
     outer = bit_list(lax.axis_size("dp"))[1:]
     total = keep.astype(f32) + flip(send.astype(bf16), "dp", 1).astype(f32)
     return reduce_outer({2 * k: total[k] for k in range(total.shape[0])}, outer)
-
-
-def reduce_halves(keep, send):
-    outer = bit_list(lax.axis_size("dp"))[1:]
-    total = keep.astype(f32) + flip(send, "dp", 1).astype(f32)
-    half = keep.shape[1] // 2
-    chunks = range(keep.shape[0])
-    low = reduce_outer({2 * k: total[k, :half] for k in chunks}, outer)
-    high = reduce_outer({2 * k: total[k, half:] for k in chunks}, outer[::-1])
-    return scatter_sum([low[r] for r in range(half)] + [high[r] for r in range(half)])
 
 
 VMEM_LIMIT = 60 * 1024 * 1024
@@ -261,36 +259,21 @@
 
 
 def backward_kernel(
-    where_ref, gres_ref, resid_ref, scale_ref, gate_ref, out_ref, cond_ref, mod_ref, gc_ref, pre_ref,
-    a0_ref, a1_ref, a2_ref, in_ref, outw_ref, *rest, split,
+    gres_ref, resid_ref, scale_ref, gate_ref, out_ref, turned_ref, mod_ref, gc_ref, pre_ref,
+    a0_ref, a1_ref, a2_ref, in_ref, outw_ref, *rest,
 ):
-    if split:
-        gnext_ref, gcn_ref, keep_ref, send_ref, normal_s, branch_s, gmi_s, dio_s = rest
-        grad_ref = keep_ref
-    else:
-        gnext_ref, gcn_ref, grad_ref, normal_s, branch_s, gmi_s, dio_s = rest[-7:]
+    gnext_ref, gcn_ref, grad_ref, normal_s, branch_s, gmi_s, dio_s, modt_s, brancht_s = rest[-9:]
     s = pl.program_id(0)
     t = pl.num_programs(0) // 2
     hid = pre_ref.shape[1]
-    d = where_ref[0]
-
-    def put(k, value):
-        c = grad_ref.shape[3]
-        if not split:
-            grad_ref[:, 0, k] = value.reshape(grad_ref.shape[0], c, hid)
-            return
-        value = value.reshape(2 * keep_ref.shape[0], c, hid)
-        for parity in range(2):
-
-            @pl.when((d & 1) == parity)
-            def _():
-                for chunk in range(value.shape[0]):
-                    ref = keep_ref if (chunk & 1) == parity else send_ref
-                    ref[(d ^ chunk) >> 1, 0, k] = value[chunk]
+    piece = (grad_ref.shape[0], grad_ref.shape[3], hid)
 
     @pl.when(s == 0)
     def _():
-        branch_s[...] = (gate_ref[...] * gres_ref[...]).astype(bf16)
+        branch = gate_ref[...] * gres_ref[...]
+        branch_s[...] = branch.astype(bf16)
+        brancht_s[...] = branch.astype(bf16).T
+        modt_s[...] = mod_ref[...].T
         gmi_s[...] = jnp.zeros_like(gmi_s)
         gcn_ref[...] = gc_ref[...]
 
@@ -300,8 +283,8 @@
         act, slope = silu_pair(pre_ref[...])
         grad_pre = (grad_act * slope).astype(bf16)
         gmi_s[...] += product_nt(grad_pre, weight(in_ref))
-        dio_s[s, 0] = product_tn(mod_ref[...], grad_pre).astype(bf16)
-        dio_s[s, 1] = product_tn(branch_s[...], act.astype(bf16)).astype(bf16)
+        dio_s[s, 0] = product(modt_s[...], grad_pre).astype(bf16)
+        dio_s[s, 1] = product(brancht_s[...], act.astype(bf16)).astype(bf16)
 
     @pl.when(s == t - 1)
     def _():
@@ -322,72 +305,60 @@
         )
         back = None
         for k, ref in enumerate((a0_ref, a1_ref, a2_ref)):
-            put(k, product_tn(cond_ref[...], grad_mods[k]).astype(bf16))
+            grad_ref[:, 0, k] = product(turned_ref[...], grad_mods[k]).astype(bf16).reshape(piece)
             term = product_nt(grad_mods[k], weight(ref))
             back = term if back is None else back + term
         gcn_ref[...] += back
         for k in range(2):
-            put(3 + k, dio_s[s - t, k])
-
-
-def layer_backward(where, grad_resid, saved, cond, grad_cond, pack, first, grads, place, count):
+            grad_ref[:, 0, 3 + k] = dio_s[s - t, k].reshape(piece)
+
+
+def layer_backward(grad_resid, saved, turned, grad_cond, pack, first, grads, place, count):
     resid, scale, gate, pre, mod, out = saved
     rows = resid.shape[0]
     n, t, _, c, hid = pack.shape
-    split = count == 0
     early = lambda s: jnp.minimum(s, t - 1)
     late = lambda s: jnp.maximum(s - t, 0)
     full = jax.ShapeDtypeStruct((rows, HW), f32)
     held = [] if grads is None else [grads]
-
-    def resident(shape, **kw):
-        return pl.BlockSpec(shape, lambda s, where: (0,) * len(shape), **kw)
-
-    def weights(k, block):
-        return pl.BlockSpec((n, 1, 1, c, hid), lambda s, where: (0, block(s), first + k, 0, 0))
-
-    if split:
-        pack_out = [
-            pl.BlockSpec((n // 2, 1, 5, c, hid), lambda s, where: (0, late(s) ^ where[1], 0, 0, 0))
-        ] * 2
-        pack_shape = [jax.ShapeDtypeStruct((n // 2, t, 5, c, hid), bf16)] * 2
-    else:
-        pack_out = [
-            pl.BlockSpec((n, 1, 5, c, hid), lambda s, where: (0, late(s), place, 0, 0))
-        ]
-        pack_shape = [jax.ShapeDtypeStruct((n, t, 5 * count, c, hid), bf16)]
+    blocks = 5 * count if grads is None else grads.shape[2]
     return pl.pallas_call(
-        partial(backward_kernel, split=split),
-        grid_spec=pltpu.PrefetchScalarGridSpec(
-            num_scalar_prefetch=1,
-            grid=(2 * t,),
-            in_specs=[resident((rows, HW), pipeline_mode=pl.Buffered(1))] * 8
-            + [pl.BlockSpec((rows, hid), lambda s, where: (0, early(s)))]
-            + [weights(k, late) for k in range(3)]
-            + [weights(k, early) for k in (3, 4)]
-            + [pl.BlockSpec(memory_space=pl.ANY)] * len(held),
-            out_specs=[resident((rows, HW)), resident((rows, HW))] + pack_out,
-            scratch_shapes=[
-                pltpu.VMEM((rows, HW), f32),
-                pltpu.VMEM((rows, HW), bf16),
-                pltpu.VMEM((rows, HW), f32),
-                pltpu.VMEM((t, 2, HW, hid), bf16),
-            ],
-        ),
-        out_shape=[full, full] + pack_shape,
-        input_output_aliases={15: 2} if held else {},
+        backward_kernel,
+        grid=(2 * t,),
+        in_specs=[whole((rows, HW))] * 5
+        + [whole((HW, rows))]
+        + [whole((rows, HW))] * 2
+        + [pl.BlockSpec((rows, hid), lambda s: (0, early(s)))]
+        + [pack_spec(pack, first + k, late) for k in range(3)]
+        + [pack_spec(pack, first + k, early) for k in (3, 4)]
+        + [pl.BlockSpec(memory_space=pl.ANY)] * len(held),
+        out_specs=[
+            out_whole((rows, HW)),
+            out_whole((rows, HW)),
+            pl.BlockSpec((n, 1, 5, c, hid), lambda s: (0, late(s), place, 0, 0)),
+        ],
+        out_shape=[full, full, jax.ShapeDtypeStruct((n, t, blocks, c, hid), bf16)],
+        input_output_aliases={14: 2} if held else {},
+        scratch_shapes=[
+            pltpu.VMEM((rows, HW), f32),
+            pltpu.VMEM((rows, HW), bf16),
+            pltpu.VMEM((rows, HW), f32),
+            pltpu.VMEM((t, 2, HW, hid), bf16),
+            pltpu.VMEM((HW, rows), bf16),
+            pltpu.VMEM((HW, rows), bf16),
+        ],
         compiler_params=params(),
-        cost_estimate=cost(4 * rows * HW * 5 * HW, 20 * HW * HW + 40 * rows * HW),
-    )(where, grad_resid, resid, scale, gate, out, cond, mod, grad_cond, pre, *[pack] * 5, *held)
+        cost_estimate=cost(rows, rows),
+    )(grad_resid, resid, scale, gate, out, turned, mod, grad_cond, pre, *[pack] * 5, *held)
 
 
 def final_kernel(
-    resid_ref, cond_ref, eps_ref, coef_ref, wm_ref, wv_ref, f0_ref, f1_ref,
+    resid_ref, cond_ref, eps_ref, coef_ref, wm_ref, wv_ref, f0_ref, f1_ref, fb_ref,
     gres_ref, gc_ref, grad_ref, loss_ref, dm_ref, dv_ref,
     scale_s, shift_s, normal_s, gfin_s,
 ):
     s = pl.program_id(0)
-    t = pl.num_programs(0) // 2
+    t = pl.num_programs(0) // 3
     hid = f0_ref.shape[4]
     piece = (grad_ref.shape[0], grad_ref.shape[3], hid)
 
@@ -436,26 +407,23 @@
 
     @pl.when(s >= t)
     def _():
-        cols = pl.ds(pl.multiple_of((s - t) * hid, hid), hid)
-        grad_fin = gfin_s[:, cols]
-        grad_mods = (grad_fin.astype(bf16), (grad_fin * normal_s[:, cols]).astype(bf16))
-        for k, ref in enumerate((f0_ref, f1_ref)):
-            grad_ref[:, 0, k] = (
-                product_tn(cond_ref[...], grad_mods[k]).astype(bf16).reshape(piece)
-            )
-            gc_ref[...] += product_nt(grad_mods[k], weight(ref))
-
-
-def final_layer(resid, cond, eps_true, coefs, w_mean, w_var, pack, first):
+        cols = pl.ds(pl.multiple_of(((s - t) >> 1) * hid, hid), hid)
+        factor = jnp.where(((s - t) & 1) == 0, 1.0, normal_s[:, cols])
+        grad_mod = (gfin_s[:, cols] * factor).astype(bf16)
+        grad_ref[:, 0, 0] = product_tn(cond_ref[...], grad_mod).astype(bf16).reshape(piece)
+        gc_ref[...] += product_nt(grad_mod, weight(fb_ref))
+
+
+def final_layer(resid, cond, eps_true, coefs, w_mean, w_var, pack, first, place):
     rows = resid.shape[0]
     n, t, _, c, hid = pack.shape
     full = jax.ShapeDtypeStruct((rows, HW), f32)
     thin = jax.ShapeDtypeStruct((HW, TOKCH), f32)
-    both = lambda s: jnp.where(s < t, s, s - t)
+    early = lambda s: jnp.minimum(s, t - 1)
     late = lambda s: jnp.maximum(s - t, 0)
     return pl.pallas_call(
         final_kernel,
-        grid=(2 * t,),
+        grid=(3 * t,),
         in_specs=[
             whole((rows, HW)),
             whole((rows, HW)),
@@ -464,11 +432,18 @@
             whole((HW, TOKCH)),
             whole((HW, TOKCH)),
         ]
-        + [pack_spec(pack, first + k, both) for k in range(2)],
+        + [pack_spec(pack, first + k, early) for k in range(2)]
+        + [
+            pl.BlockSpec(
+                (n, 1, 1, c, hid), lambda s: (0, late(s) >> 1, first + (late(s) & 1), 0, 0)
+            )
+        ],
         out_specs=[
             out_whole((rows, HW)),
             out_whole((rows, HW)),
-            pl.BlockSpec((n, 1, 2, c, hid), lambda s: (0, late(s), 0, 0, 0)),
+            pl.BlockSpec(
+                (n, 1, 1, c, hid), lambda s: (0, late(s) >> 1, place + (late(s) & 1), 0, 0)
+            ),
             out_whole((8, 128)),
             out_whole((HW, TOKCH)),
             out_whole((HW, TOKCH)),
@@ -476,7 +451,7 @@
         out_shape=[
             full,
             full,
-            jax.ShapeDtypeStruct((n, t, 2, c, hid), bf16),
+            jax.ShapeDtypeStruct((n, t, place + 2, c, hid), bf16),
             jax.ShapeDtypeStruct((8, 128), f32),
             thin,
             thin,
@@ -484,7 +459,7 @@
         scratch_shapes=[pltpu.VMEM((rows, HW), f32)] * 4,
         compiler_params=params(),
         cost_estimate=cost(6 * rows * HW * 2 * HW, 8 * HW * HW + 20 * rows * HW),
-    )(resid, cond, eps_true, coefs, w_mean, w_var, pack, pack)
+    )(resid, cond, eps_true, coefs, w_mean, w_var, *[pack] * 3)
 
 
 def condition_kernel(
@@ -556,7 +531,7 @@
         ],
         scratch_shapes=[pltpu.VMEM((rows, HW), f32)],
         compiler_params=params(),
-        cost_estimate=cost(4 * rows * HW * 2 * HW, 10 * HW * HW + 20 * rows * HW),
+        cost_estimate=cost(rows, rows),
     )(
         grad_cond, condition, time_pre, time_act, embedded, cond_in, time_out_weight,
         cond_weight,
@@ -722,30 +697,20 @@
         out_full[:, TOKCH:],
         second_pack,
         5 * (DEPTH - half_depth),
+        0,
     )
     loss_total = loss_tile[0, 0]
     out_weight_part = jnp.concatenate([mean_part, var_part], axis=1)
 
-    final_grad = jnp.moveaxis(reduce_pack(final_grads, z), 0, 1)
-    where = jnp.stack([d, z]).astype(jnp.int32)
-    reds = [None] * DEPTH
-    grads = None
-    for l in reversed(range(half_depth, DEPTH)):
-        grad_resid, grad_cact, grads = layer_backward(
-            where, grad_resid, stored[l], cond_act, grad_cact, *pack_of(l),
-            grads, l - half_depth, DEPTH - half_depth,
-        )
-    summed = reduce_pack(grads, z)
-    for l in range(half_depth, DEPTH):
-        reds[l] = summed[5 * (l - half_depth) : 5 * (l - half_depth) + 5]
-    for l in reversed(range(half_depth)):
-        grad_resid, grad_cact, keep, send = layer_backward(
-            where, grad_resid, stored[l], cond_act, grad_cact, *pack_of(l), None, 0, 0
-        )
-        reds[l] = reduce_halves(keep, send)
-    ada_grad = jnp.stack([jnp.moveaxis(red[:3], 0, 1) for red in reds])
-    in_grad = jnp.stack([red[3] for red in reds])
-    out_grad = jnp.stack([red[4].T for red in reds])
+    cond_turned = cond_act.T
+    buffers = []
+    for group in GROUPS:
+        grads = None
+        for i, l in enumerate(group):
+            grad_resid, grad_cact, grads = layer_backward(
+                grad_resid, stored[l], cond_turned, grad_cact, *pack_of(l), grads, i, len(group)
+            )
+        buffers.append(grads)
     input_weight_part = product_tn(noisy_rows, grad_resid.astype(bf16))
 
     grad_cond_in, *thin = condition_backward(
@@ -804,6 +769,19 @@
     input_grad = relabel(
         jnp.concatenate(gather_blocks(input_own.astype(bf16)), axis=0), 0, t, z
     ).astype(f32)
+
+    final_part = reduce_over_dp(final_grads)
+    final_grad = jnp.moveaxis(reduce_tensor(final_part, z), 0, 1)
+    parts = [reduce_over_dp(buffers[0])]
+    parts += [reduce_over_dp(after(buffer, parts[0], query_grad)) for buffer in buffers[1:]]
+    reds = [None] * DEPTH
+    for group, part in zip(GROUPS, parts):
+        group_sum = reduce_tensor(part, z)
+        for i, l in enumerate(group):
+            reds[l] = group_sum[5 * i : 5 * i + 5]
+    ada_grad = jnp.stack([jnp.moveaxis(red[:3], 0, 1) for red in reds])
+    in_grad = jnp.stack([red[3] for red in reds])
+    out_grad = jnp.stack([red[4].T for red in reds])
 
     whole_grads = jnp.concatenate(
         [

time: 1290 us -> 1190 us (0.922)
  waiting for transfers between devices: 646 us -> 590 us
  other arithmetic: 117 us -> 68.2 us
  local copies, waits for them, and re-layouts: 108 us -> 126 us
  Pallas kernels: 264 us -> 250 us
    ppermute x79 -> x58, waiting for transfers between devices: 439 us -> 348 us  [flip(): return lax.ppermute(values, axis, [(i, i ^ mask) for i in range(size)])]
    another operation x10 -> x3, other arithmetic: 55.3 us -> 13 us
    reduce_scatter x2 -> x3, waiting for transfers between devices: 0.04 us -> 38 us  [reduce_over_dp(): return lax.psum_scatter(grads, 'dp', scatter_dimension=0, tiled=True)[0]]
    pallas_call x7, Pallas kernels: 169 us -> 155 us  [the longest x6 138 us: layer_backward(): pl.pallas_call(backward_kernel, grid=(2 * t,), in_specs=[whole((rows, HW)...]
    unnamed x277 -> x261, local copies, waits for them, and re-layouts: 42.2 us -> 54.1 us
    ppermute x79 -> x58, starting transfers between devices: 93.7 us -> 88.8 us  [flip(): return lax.ppermute(values, axis, [(i, i ^ mask) for i in range(size)])]
  transfers between devices with their start and end apart: 83 -> 63, of which waited for: 43 -> 34; matrix products, arithmetic and copies ran while one was open for 18% -> 16% of each run, Pallas kernels for 16% -> 11%
where the time goes in v2:
time: 1190 us; the launch traced here: 1180 us
  waiting for transfers between devices  590 us (50%)
  Pallas kernels  250 us (21%)
  local copies, waits for them, and re-layouts  126 us (11%)
  starting transfers between devices  89 us (7%)
  other arithmetic  68.2 us (6%)
  matrix products  38.7 us (3%)
  between operations  17.7 us (1%)
    ppermute x58, waiting for transfers between devices, flip(): return lax.ppermute(values, axis, [(i, i ^ mask) for i in range(size)])  348 us
    all_gather x2, waiting for transfers between devices, gather_pack(): full = lax.all_gather(chunk, ('dp', 'tensor'), axis=0, tiled=False)  204 us
    pallas_call x6, Pallas kernels, layer_backward(): pl.pallas_call(backward_kernel, grid=(2 * t,), in_specs=[whole((rows, HW)...  138 us
    ppermute x58, starting transfers between devices, flip(): return lax.ppermute(values, axis, [(i, i ^ mask) for i in range(size)])  88.8 us
    pallas_call x6, Pallas kernels, layer_forward(): pl.pallas_call(forward_kernel, grid=(2 * t,), in_specs=[whole((rows, HW))...  81.6 us
    unnamed x261, local copies, waits for them, and re-layouts  54.1 us
    reduce_scatter x3, waiting for transfers between devices, reduce_over_dp(): return lax.psum_scatter(grads, 'dp', scatter_dimension=0, tiled=True)[0]  38 us
  transfers between devices with their start and end apart: 63, of which 34 were waited for; matrix products, arithmetic and copies ran while one was open for 16% of the time, Pallas kernels for 11%

profile of v2, /device:TPU:0, one launch (start us, length us, event | category | flops | bytes accessed | tf_op | source)
XLA Modules:
  0.0 1180.4 jit_solution(7521093710196574525)
XLA Ops:
  68.2 35.9 %collective-permute-done.4 = bf16[128,768]{1,0:T(8,128)(2,1)S(1)} collective-permute-done((bf16[128,768]{1,0:T(8,128)(2,1)S(1)}, bf16[128,768]{1,0:T(8,128)(2,1)S(1)}, u32[]{:S(2)}, u32[]{:S(2)}) %collective-permute-start.4) | collective-permute-done | bytes 196640 | tf_op jit(solution)/shard_map/ppermute | solution.py:46
  117.3 14.9 %collective-permute-done.7 = bf16[128,768]{1,0:T(8,128)(2,1)S(1)} collective-permute-done((bf16[128,768]{1,0:T(8,128)(2,1)S(1)}, bf16[128,768]{1,0:T(8,128)(2,1)S(1)}, u32[]{:S(2)}, u32[]{:S(2)}) %collective-permute-start.7) | collective-permute-done | bytes 196640 | tf_op jit(solution)/shard_map/ppermute | solution.py:46
  142.4 7.9 collective-permute-done.9
  150.3 31.1 %collective-permute-done.10 = bf16[128,768]{1,0:T(8,128)(2,1)S(1)} collective-permute-done((bf16[128,768]{1,0:T(8,128)(2,1)S(1)}, bf16[128,768]{1,0:T(8,128)(2,1)S(1)}, u32[]{:S(2)}, u32[]{:S(2)}) %collective-permute-start.10) | collective-permute-done | bytes 196640 | tf_op jit(solution)/shard_map/ppermute | solution.py:46
  193.2 18.0 %collective-permute-done.13 = bf16[128,768]{1,0:T(8,128)(2,1)S(1)} collective-permute-done((bf16[128,768]{1,0:T(8,128)(2,1)S(1)}, bf16[128,768]{1,0:T(8,128)(2,1)S(1)}, u32[]{:S(2)}, u32[]{:S(2)}) %collective-permute-start.13) | collective-permute-done | bytes 196640 | tf_op jit(solution)/shard_map/ppermute | solution.py:46
  220.3 37.1 %all-gather.5.cloned.1.call-done = bf16[480,128,256]{2,1,0:T(8,128)(2,1)} async-done(((bf16[15,128,256]{2,1,0:T(8,128)(2,1)}), bf16[480,128,256]{2,1,0:T(8,128)(2,1)}) %all-gather.5.cloned.1.call-update) | async-done | bytes 31457296 | tf_op jit(solution)/shard_map/all_gather | solution.py:129
  257.4 13.5 %shard_map.384 = (f32[320,1024]{1,0:T(8,128)}, f32[320,1024]{1,0:T(8,128)}, f32[320,1024]{1,0:T(8,128)}, bf16[320,1024]{1,0:T(8,128)(2,1)}, f32[320,1024]{1,0:T(8,128)}, /*index=5*/f32[320,1024]{1,0:T(8,128)}) custom-call(f32[320,1024]{1,0:T(8,128)} %fusion.87.resid_ref, bf16[320,1024]{1,0:T(8,128)(2,1)} %get-tuple-element.89.cond_ref, ...), custom_call_target="tpu_custom_call" | custom-call | flops 3355443200 | bytes 20316160 | tf_op jit(solution)/shard_map/pallas_call | solution.py:240
  270.9 13.5 %shard_map.385 = (f32[320,1024]{1,0:T(8,128)}, f32[320,1024]{1,0:T(8,128)}, f32[320,1024]{1,0:T(8,128)}, bf16[320,1024]{1,0:T(8,128)(2,1)}, f32[320,1024]{1,0:T(8,128)}, /*index=5*/f32[320,1024]{1,0:T(8,128)}) custom-call(f32[320,1024]{1,0:T(8,128)} %get-tuple-element.90.resid_ref, bf16[320,1024]{1,0:T(8,128)(2,1)} %get-tuple-element.89.cond_ref, ...), custom_call_target="tpu_custom_call" | custom-call | flops 3355443200 | bytes 20316160 | tf_op jit(solution)/shard_map/pallas_call | solution.py:240
  284.4 13.6 %shard_map.386 = (f32[320,1024]{1,0:T(8,128)}, f32[320,1024]{1,0:T(8,128)}, f32[320,1024]{1,0:T(8,128)}, bf16[320,1024]{1,0:T(8,128)(2,1)}, f32[320,1024]{1,0:T(8,128)}, /*index=5*/f32[320,1024]{1,0:T(8,128)}) custom-call(f32[320,1024]{1,0:T(8,128)} %get-tuple-element.91.resid_ref, bf16[320,1024]{1,0:T(8,128)(2,1)} %get-tuple-element.89.cond_ref, ...), custom_call_target="tpu_custom_call" | custom-call | flops 3355443200 | bytes 20316160 | tf_op jit(solution)/shard_map/pallas_call | solution.py:240
  298.0 167.1 %all-gather.7.cloned.1.call-done = bf16[544,128,256]{2,1,0:T(8,128)(2,1)} async-done(((bf16[17,128,256]{2,1,0:T(8,128)(2,1)}), bf16[544,128,256]{2,1,0:T(8,128)(2,1)}) %all-gather.7.cloned.1.call-update) | async-done | bytes 35651600 | tf_op jit(solution)/shard_map/all_gather | solution.py:129
  465.1 13.7 %shard_map.387 = (f32[320,1024]{1,0:T(8,128)}, f32[320,1024]{1,0:T(8,128)}, f32[320,1024]{1,0:T(8,128)}, bf16[320,1024]{1,0:T(8,128)(2,1)}, f32[320,1024]{1,0:T(8,128)}, /*index=5*/f32[320,1024]{1,0:T(8,128)}) custom-call(f32[320,1024]{1,0:T(8,128)} %get-tuple-element.92.resid_ref, bf16[320,1024]{1,0:T(8,128)(2,1)} %get-tuple-element.89.cond_ref, ...), custom_call_target="tpu_custom_call" | custom-call | flops 3355443200 | bytes 20316160 | tf_op jit(solution)/shard_map/pallas_call | solution.py:240
  478.8 13.7 %shard_map.388 = (f32[320,1024]{1,0:T(8,128)}, f32[320,1024]{1,0:T(8,128)}, f32[320,1024]{1,0:T(8,128)}, bf16[320,1024]{1,0:T(8,128)(2,1)}, f32[320,1024]{1,0:T(8,128)}, /*index=5*/f32[320,1024]{1,0:T(8,128)}) custom-call(f32[320,1024]{1,0:T(8,128)} %get-tuple-element.93.resid_ref, bf16[320,1024]{1,0:T(8,128)(2,1)} %get-tuple-element.89.cond_ref, ...), custom_call_target="tpu_custom_call" | custom-call | flops 3355443200 | bytes 20316160 | tf_op jit(solution)/shard_map/pallas_call | solution.py:240
  492.5 13.6 %shard_map.389 = (f32[320,1024]{1,0:T(8,128)}, f32[320,1024]{1,0:T(8,128)}, f32[320,1024]{1,0:T(8,128)}, bf16[320,1024]{1,0:T(8,128)(2,1)}, f32[320,1024]{1,0:T(8,128)}, /*index=5*/f32[320,1024]{1,0:T(8,128)}) custom-call(f32[320,1024]{1,0:T(8,128)} %get-tuple-element.94.resid_ref, bf16[320,1024]{1,0:T(8,128)(2,1)} %get-tuple-element.89.cond_ref, ...), custom_call_target="tpu_custom_call" | custom-call | flops 3355443200 | bytes 20316160 | tf_op jit(solution)/shard_map/pallas_call | solution.py:240
  506.1 17.0 %shard_map.390 = (f32[320,1024]{1,0:T(8,128)}, f32[320,1024]{1,0:T(8,128)}, bf16[8,4,2,128,256]{4,3,2,1,0:T(8,128)(2,1)}, f32[8,128]{1,0:T(8,128)}, f32[1024,16]{1,0:T(8,128)}, /*index=5*/f32[1024,16]{1,0:T(8,128)}) custom-call(f32[320,1024]{1,0:T(8,128)} %get-tuple-element.95.resid_ref, bf16[320,1024]{1,0:T(8,128)(2,1)} %get-tuple-element.89.cond_ref, ...), custom_call_target="tpu_custom_call" | custom-call | flops 4026531840 | bytes 14942208 | tf_op jit(solution)/shard_map/pallas_call | solution.py:424
  523.1 22.2 %shard_map.391 = (f32[320,1024]{1,0:T(8,128)}, f32[320,1024]{1,0:T(8,128)}, bf16[8,4,15,128,256]{4,3,2,1,0:T(8,128)(2,1)}) custom-call(f32[320,1024]{1,0:T(8,128)} %get-tuple-element.96.gres_ref, f32[320,1024]{1,0:T(8,128)} %get-tuple-element.94.resid_ref, f32[320,1024]{1,0:T(8,128)} %get-tuple-element.97.scale_ref, f32[320,1024]{1,0:T(8,128)} %get-tuple-element.98.gate_ref, ...), custom_call_target="tpu_custom_call" | custom-call | flops 320 | bytes 320 | tf_op jit(solution)/shard_map/pallas_call | solution.py:325
  545.3 21.8 %shard_map.392 = (f32[320,1024]{1,0:T(8,128)}, f32[320,1024]{1,0:T(8,128)}, bf16[8,4,15,128,256]{4,3,2,1,0:T(8,128)(2,1)}) custom-call(f32[320,1024]{1,0:T(8,128)} %get-tuple-element.103.gres_ref, f32[320,1024]{1,0:T(8,128)} %get-tuple-element.93.resid_ref, f32[320,1024]{1,0:T(8,128)} %get-tuple-element.104.scale_ref, ...), custom_call_target="tpu_custom_call", output_to_operand_aliasing={{2}: (14, {})} | custom-call | flops 320 | bytes 320 | tf_op jit(solution)/shard_map/pallas_call | solution.py:325
  567.1 22.0 %shard_map.393 = (f32[320,1024]{1,0:T(8,128)}, f32[320,1024]{1,0:T(8,128)}, bf16[8,4,15,128,256]{4,3,2,1,0:T(8,128)(2,1)}) custom-call(f32[320,1024]{1,0:T(8,128)} %get-tuple-element.111.gres_ref, f32[320,1024]{1,0:T(8,128)} %get-tuple-element.92.resid_ref, f32[320,1024]{1,0:T(8,128)} %get-tuple-element.112.scale_ref, ...), custom_call_target="tpu_custom_call", output_to_operand_aliasing={{2}: (14, {})} | custom-call | flops 320 | bytes 320 | tf_op jit(solution)/shard_map/pallas_call | solution.py:325
  589.7 24.3 %shard_map.394 = (f32[320,1024]{1,0:T(8,128)}, f32[320,1024]{1,0:T(8,128)}, bf16[8,4,15,128,256]{4,3,2,1,0:T(8,128)(2,1)}) custom-call(f32[320,1024]{1,0:T(8,128)} %get-tuple-element.119.gres_ref, f32[320,1024]{1,0:T(8,128)} %get-tuple-element.91.resid_ref, f32[320,1024]{1,0:T(8,128)} %get-tuple-element.120.scale_ref, ...), custom_call_target="tpu_custom_call" | custom-call | flops 320 | bytes 320 | tf_op jit(solution)/shard_map/pallas_call | solution.py:325
  614.0 25.4 %shard_map.395 = (f32[320,1024]{1,0:T(8,128)}, f32[320,1024]{1,0:T(8,128)}, bf16[8,4,15,128,256]{4,3,2,1,0:T(8,128)(2,1)}) custom-call(f32[320,1024]{1,0:T(8,128)} %get-tuple-element.126.gres_ref, f32[320,1024]{1,0:T(8,128)} %get-tuple-element.90.resid_ref, f32[320,1024]{1,0:T(8,128)} %get-tuple-element.127.scale_ref, ...), custom_call_target="tpu_custom_call", output_to_operand_aliasing={{2}: (14, {})} | custom-call | flops 320 | bytes 320 | tf_op jit(solution)/shard_map/pallas_call | solution.py:325
  639.3 22.1 %shard_map.396 = (f32[320,1024]{1,0:T(8,128)}, f32[320,1024]{1,0:T(8,128)}, bf16[8,4,15,128,256]{4,3,2,1,0:T(8,128)(2,1)}) custom-call(f32[320,1024]{1,0:T(8,128)} %get-tuple-element.134.gres_ref, f32[320,1024]{1,0:T(8,128)} %fusion.87.resid_ref, f32[320,1024]{1,0:T(8,128)} %get-tuple-element.135.scale_ref, ...), custom_call_target="tpu_custom_call", output_to_operand_aliasing={{2}: (14, {})} | custom-call | flops 320 | bytes 320 | tf_op jit(solution)/shard_map/pallas_call | solution.py:325
  661.5 8.7 shard_map.397
  703.6 8.1 collective-permute-done.22
  814.4 8.5 collective-permute-done.28
  879.1 9.9 collective-permute-done.39
  892.7 18.2 %collective-permute-done.42 = bf16[2,96,2304]{2,1,0:T(8,128)(2,1)} collective-permute-done((bf16[2,96,2304]{2,1,0:T(8,128)(2,1)}, bf16[2,96,2304]{2,1,0:T(8,128)(2,1)}, u32[]{:S(2)}, u32[]{:S(2)}) %collective-permute-start.42) | collective-permute-done | bytes 884768 | tf_op jit(solution)/shard_map/ppermute | solution.py:46
  930.7 14.5 %collective-permute-done.43 = bf16[1,96,2304]{2,1,0:T(8,128)(2,1)S(1)} collective-permute-done((bf16[1,96,2304]{2,1,0:T(8,128)(2,1)}, bf16[1,96,2304]{2,1,0:T(8,128)(2,1)S(1)}, u32[]{:S(2)}, u32[]{:S(2)}) %collective-permute-start.43) | collective-permute-done | bytes 442400 | tf_op jit(solution)/shard_map/ppermute | solution.py:46
  963.4 9.8 collective-permute-done.48
  975.4 32.6 %collective-permute-done.55 = bf16[2,128,256]{2,1,0:T(8,128)(2,1)} collective-permute-done((bf16[2,128,256]{2,1,0:T(8,128)(2,1)}, bf16[2,128,256]{2,1,0:T(8,128)(2,1)}, u32[]{:S(2)}, u32[]{:S(2)}) %collective-permute-start.55) | collective-permute-done | bytes 131104 | tf_op jit(solution)/shard_map/ppermute | solution.py:46
  1008.1 38.0 %reduce-scatter.4.cloned.1.call-done = bf16[1,4,15,128,256]{4,3,2,1,0:T(8,128)(2,1)} async-done(((bf16[8,4,15,128,256]{4,3,2,1,0:T(8,128)(2,1)}), bf16[1,4,15,128,256]{4,3,2,1,0:T(8,128)(2,1)}) %reduce-scatter.4.cloned.1.call-update) | async-done | bytes 3932176 | tf_op jit(solution)/shard_map/reduce_scatter | solution.py:134
  1048.1 18.3 %collective-permute-start.49 = (bf16[15,128,256]{2,1,0:T(8,128)(2,1)S(1)}, bf16[15,128,256]{2,1,0:T(8,128)(2,1)S(1)}, u32[]{:S(2)}, u32[]{:S(2)}) collective-permute-start(bf16[15,128,256]{2,1,0:T(8,128)(2,1)S(1)} %get-tuple-element.251), channel_id=1, source_target_pairs={{0,1},{1,0},{2,3},{3,2},{4,5},{5,4},{6,7},{7,6},{8,9},{9,8},{10,11... | collective-permute-start | bytes 2949128 | tf_op jit(solution)/shard_map/ppermute | solution.py:46
  1078.7 28.3 %collective-permute-done.49 = bf16[15,128,256]{2,1,0:T(8,128)(2,1)S(1)} collective-permute-done((bf16[15,128,256]{2,1,0:T(8,128)(2,1)S(1)}, bf16[15,128,256]{2,1,0:T(8,128)(2,1)S(1)}, u32[]{:S(2)}, u32[]{:S(2)}) %collective-permute-start.49) | collective-permute-done | bytes 983072 | tf_op jit(solution)/shard_map/ppermute | solution.py:46
  1112.4 39.6 %collective-permute-done.50 = bf16[15,128,256]{2,1,0:T(8,128)(2,1)S(1)} collective-permute-done((bf16[15,128,256]{2,1,0:T(8,128)(2,1)S(1)}, bf16[15,128,256]{2,1,0:T(8,128)(2,1)S(1)}, u32[]{:S(2)}, u32[]{:S(2)}) %collective-permute-start.50) | collective-permute-done | bytes 983072 | tf_op jit(solution)/shard_map/ppermute | solution.py:46
  (548 shorter events, 380.0 us)
Async XLA Ops:
  7.2 250.2 %all-gather.5.cloned.1.call-start = ((), (), s32[]{:S(2)}) async-start(), calls=%async_computation.6 | async-start | bytes 32440320 | tf_op jit(solution)/shard_map/all_gather | solution.py:129
  18.8 446.3 %all-gather.7.cloned.1.call-start = ((), (), s32[]{:S(2)}) async-start(), calls=%async_computation.7 | async-start | bytes 36765696 | tf_op jit(solution)/shard_map/all_gather | solution.py:129
  21.1 929.1 %reduce-scatter.6.cloned.1.call-start = ((), (), s32[]{:S(2)}) async-start(), calls=%async_computation.4 | async-start | bytes 35389440 | tf_op jit(solution)/shard_map/reduce_scatter | solution.py:134
  21.2 35.5 %collective-permute-start.1 = (bf16[16,256]{1,0:T(8,128)(2,1)}, bf16[16,256]{1,0:T(8,128)(2,1)}, u32[]{:S(2)}, u32[]{:S(2)}) collective-permute-start(bf16[16,256]{1,0:T(8,128)(2,1)} %param.42), channel_id=1, source_target_pairs={{0,2},{1,3},{2,0},{3,1},{4,6},{5,7},{6,4},{7,5},{8,10},{9,11},{10,... | collective-permute-start | bytes 24584 | tf_op jit(solution)/shard_map/ppermute | solution.py:46
  25.3 30.0 %collective-permute-start = (bf16[16,256]{1,0:T(8,128)(2,1)}, bf16[16,256]{1,0:T(8,128)(2,1)}, u32[]{:S(2)}, u32[]{:S(2)}) collective-permute-start(bf16[16,256]{1,0:T(8,128)(2,1)} %param.42), channel_id=1, source_target_pairs={{0,1},{1,0},{2,3},{3,2},{4,5},{5,4},{6,7},{7,6},{8,9},{9,8},{10,11... | collective-permute-start | bytes 24584 | tf_op jit(solution)/shard_map/ppermute | solution.py:46
  26.8 32.5 %collective-permute-start.2 = (bf16[16,256]{1,0:T(8,128)(2,1)}, bf16[16,256]{1,0:T(8,128)(2,1)}, u32[]{:S(2)}, u32[]{:S(2)}) collective-permute-start(bf16[16,256]{1,0:T(8,128)(2,1)} %param.42), channel_id=1, source_target_pairs={{0,3},{1,2},{2,1},{3,0},{4,7},{5,6},{6,5},{7,4},{8,11},{9,10},{10,... | collective-permute-start | bytes 24584 | tf_op jit(solution)/shard_map/ppermute | solution.py:46
  26.8 83.3 %collective-permute-start.16 = (bf16[256,32]{0,1:T(8,128)(2,1)}, bf16[256,32]{0,1:T(8,128)(2,1)}, u32[]{:S(2)}, u32[]{:S(2)}) collective-permute-start(bf16[256,32]{0,1:T(8,128)(2,1)} %param.47), channel_id=1, source_target_pairs={{0,2},{1,3},{2,0},{3,1},{4,6},{5,7},{6,4},{7,5},{8,10},{9,11},{10,... | collective-permute-start | bytes 49160 | tf_op jit(solution)/shard_map/ppermute | solution.py:46
  28.7 36.1 %collective-permute-start.15 = (bf16[256,32]{0,1:T(8,128)(2,1)}, bf16[256,32]{0,1:T(8,128)(2,1)}, u32[]{:S(2)}, u32[]{:S(2)}) collective-permute-start(bf16[256,32]{0,1:T(8,128)(2,1)} %param.47), channel_id=1, source_target_pairs={{0,1},{1,0},{2,3},{3,2},{4,5},{5,4},{6,7},{7,6},{8,9},{9,8},{10,11... | collective-permute-start | bytes 49160 | tf_op jit(solution)/shard_map/ppermute | solution.py:46
  59.4 44.7 %collective-permute-start.4 = (bf16[128,768]{1,0:T(8,128)(2,1)S(1)}, bf16[128,768]{1,0:T(8,128)(2,1)S(1)}, u32[]{:S(2)}, u32[]{:S(2)}) collective-permute-start(bf16[128,768]{1,0:T(8,128)(2,1)S(1)} %get-tuple-element.293), channel_id=1, source_target_pairs={{0,2},{1,3},{2,0},{3,1},{4,6},{5,7},{6,4},{7,5},{8,10},{9,11},{10,... | collective-permute-start | bytes 589832 | tf_op jit(solution)/shard_map/ppermute | solution.py:46
  64.8 46.0 %collective-permute-start.17 = (bf16[256,32]{0,1:T(8,128)(2,1)}, bf16[256,32]{0,1:T(8,128)(2,1)S(1)}, u32[]{:S(2)}, u32[]{:S(2)}) collective-permute-start(bf16[256,32]{0,1:T(8,128)(2,1)} %param.47), channel_id=1, source_target_pairs={{0,3},{1,2},{2,1},{3,0},{4,7},{5,6},{6,5},{7,4},{8,11},{9,10},{10,... | collective-permute-start | bytes 49160 | tf_op jit(solution)/shard_map/ppermute | solution.py:46
  105.7 26.4 %collective-permute-start.7 = (bf16[128,768]{1,0:T(8,128)(2,1)S(1)}, bf16[128,768]{1,0:T(8,128)(2,1)S(1)}, u32[]{:S(2)}, u32[]{:S(2)}) collective-permute-start(bf16[128,768]{1,0:T(8,128)(2,1)S(1)} %add_convert_fusion.4), channel_id=1, source_target_pairs={{0,2},{1,3},{2,0},{3,1},{4,6},{5,7},{6,4},{7,5},{8,10},{9,11},{10,... | collective-permute-start | bytes 589832 | tf_op jit(solution)/shard_map/ppermute | solution.py:46
  105.8 26.4 %collective-permute-start.6 = (bf16[128,768]{1,0:T(8,128)(2,1)S(1)}, bf16[128,768]{1,0:T(8,128)(2,1)S(1)}, u32[]{:S(2)}, u32[]{:S(2)}) collective-permute-start(bf16[128,768]{1,0:T(8,128)(2,1)S(1)} %add_convert_fusion.4), channel_id=1, source_target_pairs={{0,1},{1,0},{2,3},{3,2},{4,5},{5,4},{6,7},{7,6},{8,9},{9,8},{10,11... | collective-permute-start | bytes 589832 | tf_op jit(solution)/shard_map/ppermute | solution.py:46
  141.3 40.1 %collective-permute-start.10 = (bf16[128,768]{1,0:T(8,128)(2,1)S(1)}, bf16[128,768]{1,0:T(8,128)(2,1)S(1)}, u32[]{:S(2)}, u32[]{:S(2)}) collective-permute-start(bf16[128,768]{1,0:T(8,128)(2,1)S(1)} %get-tuple-element.290), channel_id=1, source_target_pairs={{0,2},{1,3},{2,0},{3,1},{4,6},{5,7},{6,4},{7,5},{8,10},{9,11},{10,... | collective-permute-start | bytes 589832 | tf_op jit(solution)/shard_map/ppermute | solution.py:46
  184.5 26.8 %collective-permute-start.13 = (bf16[128,768]{1,0:T(8,128)(2,1)S(1)}, bf16[128,768]{1,0:T(8,128)(2,1)S(1)}, u32[]{:S(2)}, u32[]{:S(2)}) collective-permute-start(bf16[128,768]{1,0:T(8,128)(2,1)S(1)} %fusion.51), channel_id=1, source_target_pairs={{0,2},{1,3},{2,0},{3,1},{4,6},{5,7},{6,4},{7,5},{8,10},{9,11},{10,... | collective-permute-start | bytes 589832 | tf_op jit(solution)/shard_map/ppermute | solution.py:46
  184.5 26.8 %collective-permute-start.12 = (bf16[128,768]{1,0:T(8,128)(2,1)S(1)}, bf16[128,768]{1,0:T(8,128)(2,1)S(1)}, u32[]{:S(2)}, u32[]{:S(2)}) collective-permute-start(bf16[128,768]{1,0:T(8,128)(2,1)S(1)} %fusion.51), channel_id=1, source_target_pairs={{0,1},{1,0},{2,3},{3,2},{4,5},{5,4},{6,7},{7,6},{8,9},{9,8},{10,11... | collective-permute-start | bytes 589832 | tf_op jit(solution)/shard_map/ppermute | solution.py:46
  589.1 366.2 %reduce-scatter.8.cloned.1.call-start = ((), (), s32[]{:S(2)}) async-start(), calls=%async_computation.5 | async-start | bytes 4718592 | tf_op jit(solution)/shard_map/reduce_scatter | solution.py:134
  589.7 456.5 %reduce-scatter.4.cloned.1.call-start = ((), (), s32[]{:S(2)}) async-start(), calls=%async_computation.3 | async-start | bytes 35389440 | tf_op jit(solution)/shard_map/reduce_scatter | solution.py:134
  771.3 75.4 %collective-permute-start.44 = (bf16[4,256,1024]{2,1,0:T(8,128)(2,1)}, bf16[4,256,1024]{2,1,0:T(8,128)(2,1)}, u32[]{:S(2)}, u32[]{:S(2)}) collective-permute-start(bf16[4,256,1024]{2,1,0:T(8,128)(2,1)} %slice.364), channel_id=1, source_target_pairs={{0,4},{4,0},{8,12},{12,8},{16,20},{20,16},{24,28},{28,24},{1,5},{5... | collective-permute-start | bytes 6291464 | tf_op jit(solution)/shard_map/ppermute | solution.py:46
  845.2 27.4 %collective-permute-start.36 = (f32[15488]{0:T(1024)}, f32[15488]{0:T(1024)}, u32[]{:S(2)}, u32[]{:S(2)}) collective-permute-start(f32[15488]{0:T(1024)} %fusion.127), channel_id=1, source_target_pairs={{0,8},{4,12},{8,0},{12,4},{16,24},{20,28},{24,16},{28,20},{1,9},{5... | collective-permute-start | bytes 185864 | tf_op jit(solution)/shard_map/ppermute | solution.py:46
  854.7 35.4 %collective-permute-start.45 = (bf16[2,256,1024]{2,1,0:T(8,128)(2,1)}, bf16[2,256,1024]{2,1,0:T(8,128)(2,1)}, u32[]{:S(2)}, u32[]{:S(2)}) collective-permute-start(bf16[2,256,1024]{2,1,0:T(8,128)(2,1)} %pad_maximum_fusion.3), channel_id=1, source_target_pairs={{0,8},{4,12},{8,0},{12,4},{16,24},{20,28},{24,16},{28,20},{1,9},{5... | collective-permute-start | bytes 3145736 | tf_op jit(solution)/shard_map/ppermute | solution.py:46
  865.9 45.0 %collective-permute-start.42 = (bf16[2,96,2304]{2,1,0:T(8,128)(2,1)}, bf16[2,96,2304]{2,1,0:T(8,128)(2,1)}, u32[]{:S(2)}, u32[]{:S(2)}) collective-permute-start(bf16[2,96,2304]{2,1,0:T(8,128)(2,1)} %copy.133), channel_id=1, source_target_pairs={{0,8},{4,12},{8,0},{12,4},{16,24},{20,28},{24,16},{28,20},{1,9},{5... | collective-permute-start | bytes 2654216 | tf_op jit(solution)/shard_map/ppermute | solution.py:46
  878.4 48.8 %collective-permute-start.37 = (f32[15488]{0:T(1024)S(1)}, f32[15488]{0:T(1024)S(1)}, u32[]{:S(2)}, u32[]{:S(2)}) collective-permute-start(f32[15488]{0:T(1024)S(1)} %add.566), channel_id=1, source_target_pairs={{0,16},{4,20},{8,24},{12,28},{16,0},{20,4},{24,8},{28,12},{1,17},{... | collective-permute-start | bytes 185864 | tf_op jit(solution)/shard_map/ppermute | solution.py:46
  892.3 25.9 %collective-permute-start.46 = (bf16[1,256,1024]{2,1,0:T(8,128)(2,1)}, bf16[1,256,1024]{2,1,0:T(8,128)(2,1)}, u32[]{:S(2)}, u32[]{:S(2)}) collective-permute-start(bf16[1,256,1024]{2,1,0:T(8,128)(2,1)} %fusion.20), channel_id=1, source_target_pairs={{0,16},{4,20},{8,24},{12,28},{16,0},{20,4},{24,8},{28,12},{1,17},{... | collective-permute-start | bytes 1572872 | tf_op jit(solution)/shard_map/ppermute | solution.py:46
  953.7 116.0 %collective-permute-start.52 = (bf16[15,128,256]{2,1,0:T(8,128)(2,1)}, bf16[15,128,256]{2,1,0:T(8,128)(2,1)}, u32[]{:S(2)}, u32[]{:S(2)}) collective-permute-start(bf16[15,128,256]{2,1,0:T(8,128)(2,1)} %get-tuple-element.248), channel_id=1, source_target_pairs={{0,1},{1,0},{2,3},{3,2},{4,5},{5,4},{6,7},{7,6},{8,9},{9,8},{10,11... | collective-permute-start | bytes 2949128 | tf_op jit(solution)/shard_map/ppermute | solution.py:46
  957.1 50.9 %collective-permute-start.55 = (bf16[2,128,256]{2,1,0:T(8,128)(2,1)}, bf16[2,128,256]{2,1,0:T(8,128)(2,1)}, u32[]{:S(2)}, u32[]{:S(2)}) collective-permute-start(bf16[2,128,256]{2,1,0:T(8,128)(2,1)} %get-tuple-element.301), channel_id=1, source_target_pairs={{0,1},{1,0},{2,3},{3,2},{4,5},{5,4},{6,7},{7,6},{8,9},{9,8},{10,11... | collective-permute-start | bytes 393224 | tf_op jit(solution)/shard_map/ppermute | solution.py:46
  959.0 117.0 %collective-permute-start.54 = (bf16[15,128,256]{2,1,0:T(8,128)(2,1)}, bf16[15,128,256]{2,1,0:T(8,128)(2,1)}, u32[]{:S(2)}, u32[]{:S(2)}) collective-permute-start(bf16[15,128,256]{2,1,0:T(8,128)(2,1)} %get-tuple-element.249), channel_id=1, source_target_pairs={{0,3},{1,2},{2,1},{3,0},{4,7},{5,6},{6,5},{7,4},{8,11},{9,10},{10,... | collective-permute-start | bytes 2949128 | tf_op jit(solution)/shard_map/ppermute | solution.py:46
  960.7 115.3 %collective-permute-start.53 = (bf16[15,128,256]{2,1,0:T(8,128)(2,1)}, bf16[15,128,256]{2,1,0:T(8,128)(2,1)}, u32[]{:S(2)}, u32[]{:S(2)}) collective-permute-start(bf16[15,128,256]{2,1,0:T(8,128)(2,1)} %get-tuple-element.250), channel_id=1, source_target_pairs={{0,2},{1,3},{2,0},{3,1},{4,6},{5,7},{6,4},{7,5},{8,10},{9,11},{10,... | collective-permute-start | bytes 2949128 | tf_op jit(solution)/shard_map/ppermute | solution.py:46
  973.2 74.9 %collective-permute-start.57 = (bf16[2,128,256]{2,1,0:T(8,128)(2,1)}, bf16[2,128,256]{2,1,0:T(8,128)(2,1)S(1)}, u32[]{:S(2)}, u32[]{:S(2)}) collective-permute-start(bf16[2,128,256]{2,1,0:T(8,128)(2,1)} %get-tuple-element.302), channel_id=1, source_target_pairs={{0,3},{1,2},{2,1},{3,0},{4,7},{5,6},{6,5},{7,4},{8,11},{9,10},{10,... | collective-permute-start | bytes 393224 | tf_op jit(solution)/shard_map/ppermute | solution.py:46
  1008.0 59.5 %collective-permute-start.56 = (bf16[2,128,256]{2,1,0:T(8,128)(2,1)}, bf16[2,128,256]{2,1,0:T(8,128)(2,1)S(1)}, u32[]{:S(2)}, u32[]{:S(2)}) collective-permute-start(bf16[2,128,256]{2,1,0:T(8,128)(2,1)} %get-tuple-element.303), channel_id=1, source_target_pairs={{0,2},{1,3},{2,0},{3,1},{4,6},{5,7},{6,4},{7,5},{8,10},{9,11},{10,... | collective-permute-start | bytes 393224 | tf_op jit(solution)/shard_map/ppermute | solution.py:46
  1048.1 59.0 %collective-permute-start.49 = (bf16[15,128,256]{2,1,0:T(8,128)(2,1)S(1)}, bf16[15,128,256]{2,1,0:T(8,128)(2,1)S(1)}, u32[]{:S(2)}, u32[]{:S(2)}) collective-permute-start(bf16[15,128,256]{2,1,0:T(8,128)(2,1)S(1)} %get-tuple-element.251), channel_id=1, source_target_pairs={{0,1},{1,0},{2,3},{3,2},{4,5},{5,4},{6,7},{7,6},{8,9},{9,8},{10,11... | collective-permute-start | bytes 2949128 | tf_op jit(solution)/shard_map/ppermute | solution.py:46
  1067.5 44.9 %collective-permute-start.51 = (bf16[15,128,256]{2,1,0:T(8,128)(2,1)S(1)}, bf16[15,128,256]{2,1,0:T(8,128)(2,1)S(1)}, u32[]{:S(2)}, u32[]{:S(2)}) collective-permute-start(bf16[15,128,256]{2,1,0:T(8,128)(2,1)S(1)} %get-tuple-element.252), channel_id=1, source_target_pairs={{0,3},{1,2},{2,1},{3,0},{4,7},{5,6},{6,5},{7,4},{8,11},{9,10},{10,... | collective-permute-start | bytes 2949128 | tf_op jit(solution)/shard_map/ppermute | solution.py:46
  1069.8 82.2 %collective-permute-start.50 = (bf16[15,128,256]{2,1,0:T(8,128)(2,1)S(1)}, bf16[15,128,256]{2,1,0:T(8,128)(2,1)S(1)}, u32[]{:S(2)}, u32[]{:S(2)}) collective-permute-start(bf16[15,128,256]{2,1,0:T(8,128)(2,1)S(1)} %get-tuple-element.253), channel_id=1, source_target_pairs={{0,2},{1,3},{2,0},{3,1},{4,6},{5,7},{6,4},{7,5},{8,10},{9,11},{10,... | collective-permute-start | bytes 2949128 | tf_op jit(solution)/shard_map/ppermute | solution.py:46
  (127 other events, 1512.7 us)
Sparse Core Ops, SparseCore 0:
  18.9 238.3 all-gather.4
  260.2 204.8 all-gather.6
  589.2 187.9 reduce-scatter.5
  780.4 51.3 reduce-scatter.7
  835.7 210.3 reduce-scatter.3
